TPU v7x, 32 devices: a whole 2x2x4 slice. The times are simulated.
32 devices in a mesh: seq: 4 (over z), fsdp: 8 (over y, x, core).
Axes of the slice: x: 2, y: 2, z: 4, core: 2. Of those that a mesh axis runs over, the one named last changes fastest.
Arguments:
- tokens: bfloat16 [8, 3072, 768], P('fsdp', 'seq'), may hold values from -6 to 6
- w_qkv: bfloat16 [768, 2304], P('fsdp'), may hold values from -0.21875 to 0.21875
- w_out: bfloat16 [768, 768], P('fsdp'), may hold values from -6 to 6
- w_in: bfloat16 [768, 2304], P('fsdp'), may hold values from -0.21875 to 0.21875
- w_down: bfloat16 [1152, 768], P('fsdp'), may hold values from -0.1875 to 0.1875
- gain_attn: bfloat16 [768], P('fsdp'), may hold values from 0.5 to 1.5
- gain_mlp: bfloat16 [768], P('fsdp'), may hold values from 0.5 to 1.5
- lengths: int32 [8], P('fsdp'), may hold values from 2305 to 3072, as said below
- cotangent: bfloat16 [8, 3072, 768], P('fsdp', 'seq'), may hold values from -6 to 6
Outputs:
- layer_out: bfloat16 [8, 3072, 768], P('fsdp', 'seq')
- grad_tokens: bfloat16 [8, 3072, 768], P('fsdp', 'seq')
- grad_w_qkv: float32 [768, 2304], P('fsdp')
- grad_w_out: float32 [768, 768], P('fsdp')
- grad_w_in: float32 [768, 2304], P('fsdp')
- grad_w_down: float32 [1152, 768], P('fsdp')
- grad_gain_attn: float32 [768], P('fsdp')
- grad_gain_mlp: float32 [768], P('fsdp')
Inputs may be any that keep to these rules, and one draw needn't show every extreme that they name: lengths[s] is the number of valid tokens of sequence s; positions at or beyond it are padding, masked as keys. Some sequence has all 3072 valid in every draw.
All inputs are finite; a program needn't handle non-finite values.
Results may differ from a plain program's by a relative error of at most 0.015.
Values may be sent and summed in bfloat16 or wider, within the bound.
No kernel may reach another device: no remote copies, remote signals or barrier semaphores. Data moves between devices by JAX's collectives and lax.ppermute only.
A program may use at most 128 MiB of HBM per device.

v0:
```python
import math

import jax
import jax.numpy as jnp
from jax import lax
from jax.sharding import PartitionSpec as P

HEADS = 12


norm_eps = 1e-05
rope_base = 160000.0
masked_score = -1e30


def normalize(values, gain):
    centre = values - jnp.mean(values, -1, keepdims=True)
    spread = jnp.mean(centre * centre, -1, keepdims=True)
    return centre * lax.rsqrt(spread + norm_eps) * gain


def rotary(positions, half_dim):
    counter = jnp.arange(half_dim).astype(jnp.float32)
    inverse = jnp.exp(counter * (-math.log(rope_base) / half_dim))
    angles = positions[:, None] * inverse[None, :]
    return (jnp.cos(angles), jnp.sin(angles))


def turn(values, cosine, sine):
    half_dim = values.shape[-1] // 2
    lower = values[..., :half_dim]
    upper = values[..., half_dim:]
    return jnp.concatenate([lower * cosine - upper * sine, upper * cosine + lower * sine], -1)


def geglu(gate, upper):
    return jax.nn.gelu(gate, approximate=False) * upper


def outer(left, right):
    return lax.dot_general(
        left, right, (((0,), (0,)), ((), ())), preferred_element_type=jnp.float32
    )


def across(left, right):
    return lax.dot_general(
        left, right, (((1,), (1,)), ((), ())), preferred_element_type=jnp.float32
    )


def shards(tokens, w_qkv, w_out, w_in, w_down, gain_attn, gain_mlp, lengths, cotangent):
    groups = lax.axis_size("seq")
    place = lax.axis_index("seq")
    tok_rows = tokens.shape[1]
    width = tokens.shape[2]
    head_dim = width // HEADS
    local_heads = HEADS // groups
    span = tok_rows * groups
    scale = head_dim ** (-0.5)
    gathered = (
        lax.all_gather(w_qkv, "fsdp", axis=0, tiled=True),
        lax.all_gather(w_out, "fsdp", axis=0, tiled=True),
        lax.all_gather(w_in, "fsdp", axis=0, tiled=True),
        lax.all_gather(w_down, "fsdp", axis=0, tiled=True),
        lax.all_gather(gain_attn, "fsdp", axis=0, tiled=True),
        lax.all_gather(gain_mlp, "fsdp", axis=0, tiled=True),
    )
    inputs = tokens[0].astype(jnp.float32)
    first_gain = gathered[4].astype(jnp.float32)
    second_gain = gathered[5].astype(jnp.float32)
    h_first, first_norm_back = jax.vjp(normalize, inputs, first_gain)
    h_first_low = h_first.astype(jnp.bfloat16)
    joined = jnp.dot(h_first_low, gathered[0], preferred_element_type=jnp.float32)
    joined = joined.reshape(tok_rows, 3, HEADS, head_dim)
    positions = (place * tok_rows + jnp.arange(tok_rows)).astype(jnp.float32)
    cosine, sine = rotary(positions, head_dim // 2)

    def turn_pair(pair):
        return turn(pair, cosine[:, None, None, :], sine[:, None, None, :])

    turned, turn_back = jax.vjp(turn_pair, joined[:, :2])
    packed = jnp.concatenate([turned, joined[:, 2:]], 1).astype(jnp.bfloat16)
    packed = packed.reshape(tok_rows, 3, groups, local_heads * head_dim)
    spread_heads = lax.all_to_all(packed, "seq", split_axis=2, concat_axis=0, tiled=True)
    spread_heads = spread_heads.reshape(span, 3, local_heads, head_dim)
    query = spread_heads[:, 0]
    key_all = spread_heads[:, 1]
    value = spread_heads[:, 2]
    valid = jnp.arange(span) < lengths[0]
    block_rows = min(512, span)
    block_count = span // block_rows
    query_blocks = query.reshape(block_count, block_rows, local_heads, head_dim)

    def scores(query_block):
        score = (
            jnp.einsum("qhd,khd->hqk", query_block, key_all, preferred_element_type=jnp.float32)
            * scale
        )
        return jnp.where(valid[None, None, :], score, masked_score)

    def attend(query_block):
        score = scores(query_block)
        rowmax = jnp.max(score, -1, keepdims=True)
        expo = jnp.exp(score - rowmax)
        total = jnp.sum(expo, -1, keepdims=True)
        prob = (expo / total).astype(jnp.bfloat16)
        result = jnp.einsum("hqk,khd->qhd", prob, value, preferred_element_type=jnp.float32)
        return (result.astype(jnp.bfloat16), rowmax[..., 0] + jnp.log(total[..., 0]))

    mixed_blocks, log_totals = lax.map(attend, query_blocks)
    mixed_heads = mixed_blocks.reshape(span, 1, local_heads * head_dim)
    mixed = lax.all_to_all(mixed_heads, "seq", split_axis=0, concat_axis=1, tiled=True).reshape(
        tok_rows, width
    )
    resid = inputs + jnp.dot(mixed, gathered[1], preferred_element_type=jnp.float32)
    h_second, second_norm_back = jax.vjp(normalize, resid, second_gain)
    h_second_low = h_second.astype(jnp.bfloat16)
    gate_up = jnp.dot(h_second_low, gathered[2], preferred_element_type=jnp.float32)
    width_ff = gate_up.shape[1] // 2
    act, act_back = jax.vjp(geglu, gate_up[:, :width_ff], gate_up[:, width_ff:])
    act_low = act.astype(jnp.bfloat16)
    layer_out = (resid + jnp.dot(act_low, gathered[3], preferred_element_type=jnp.float32)).astype(
        jnp.bfloat16
    )
    matrices = (
        lax.all_gather(w_qkv, "fsdp", axis=0, tiled=True),
        lax.all_gather(w_out, "fsdp", axis=0, tiled=True),
        lax.all_gather(w_in, "fsdp", axis=0, tiled=True),
        lax.all_gather(w_down, "fsdp", axis=0, tiled=True),
    )
    grad_out = cotangent[0]
    grad_down = outer(act_low, grad_out)
    grad_act = across(grad_out, matrices[3])
    grad_gate, grad_upper = act_back(grad_act)
    grad_gate_up = jnp.concatenate([grad_gate, grad_upper], 1).astype(jnp.bfloat16)
    grad_in = outer(h_second_low, grad_gate_up)
    grad_h_second = across(grad_gate_up, matrices[2])
    grad_resid_norm, grad_second_gain = second_norm_back(grad_h_second)
    grad_resid = grad_out.astype(jnp.float32) + grad_resid_norm
    grad_attn = grad_resid.astype(jnp.bfloat16)
    grad_wout = outer(mixed, grad_attn)
    grad_mixed = across(grad_attn, matrices[1]).astype(jnp.bfloat16)
    grad_mixed = grad_mixed.reshape(tok_rows, groups, local_heads * head_dim)
    grad_heads = lax.all_to_all(grad_mixed, "seq", split_axis=1, concat_axis=0, tiled=True)
    grad_blocks = grad_heads.reshape(block_count, block_rows, local_heads, head_dim)

    def revisit(carry, item):
        grad_key, grad_value = carry
        query_block, grad_block, log_block = item
        prob = jnp.exp(scores(query_block) - log_block[..., None])
        prob_low = prob.astype(jnp.bfloat16)
        grad_value = grad_value + jnp.einsum(
            "hqk,qhd->khd", prob_low, grad_block, preferred_element_type=jnp.float32
        )
        grad_prob = jnp.einsum(
            "qhd,khd->hqk", grad_block, value, preferred_element_type=jnp.float32
        )
        grad_prob = lax.optimization_barrier(grad_prob.astype(jnp.bfloat16)).astype(jnp.float32)
        weighted = jnp.sum(prob * grad_prob, -1, keepdims=True)
        grad_score = (prob * (grad_prob - weighted)).astype(jnp.bfloat16)
        grad_query = (
            jnp.einsum("hqk,khd->qhd", grad_score, key_all, preferred_element_type=jnp.float32)
            * scale
        )
        grad_key = (
            grad_key
            + jnp.einsum(
                "hqk,qhd->khd", grad_score, query_block, preferred_element_type=jnp.float32
            )
            * scale
        )
        return ((grad_key, grad_value), grad_query)

    zeros_heads = jnp.zeros((span, local_heads, head_dim), jnp.float32)
    (grad_key_all, grad_value_all), grad_query_blocks = lax.scan(
        revisit, (zeros_heads, zeros_heads), (query_blocks, grad_blocks, log_totals)
    )
    grad_query_all = grad_query_blocks.reshape(span, local_heads, head_dim)
    grad_stack = jnp.stack([grad_query_all, grad_key_all, grad_value_all], 1).astype(jnp.bfloat16)
    grad_stack = grad_stack.reshape(span, 3, 1, local_heads * head_dim)
    returned = lax.all_to_all(grad_stack, "seq", split_axis=0, concat_axis=2, tiled=True)
    returned = returned.reshape(tok_rows, 3, HEADS, head_dim).astype(jnp.float32)
    (grad_unturned,) = turn_back(returned[:, :2])
    grad_joined = jnp.concatenate([grad_unturned, returned[:, 2:]], 1).reshape(tok_rows, 3 * width)
    grad_joined = grad_joined.astype(jnp.bfloat16)
    grad_wqkv = outer(h_first_low, grad_joined)
    grad_h_first = across(grad_joined, matrices[0])
    grad_input_norm, grad_first_gain = first_norm_back(grad_h_first)
    grad_tokens = (grad_resid + grad_input_norm).astype(jnp.bfloat16)
    shares = (
        lax.psum_scatter(grad_wqkv, "fsdp", scatter_dimension=0, tiled=True),
        lax.psum_scatter(grad_wout, "fsdp", scatter_dimension=0, tiled=True),
        lax.psum_scatter(grad_in, "fsdp", scatter_dimension=0, tiled=True),
        lax.psum_scatter(grad_down, "fsdp", scatter_dimension=0, tiled=True),
        lax.psum_scatter(grad_first_gain, "fsdp", scatter_dimension=0, tiled=True),
        lax.psum_scatter(grad_second_gain, "fsdp", scatter_dimension=0, tiled=True),
    )
    totals = lax.psum((shares[0], shares[1], shares[2], shares[3], shares[4], shares[5]), "seq")
    return (
        layer_out[None],
        grad_tokens[None],
        totals[0],
        totals[1],
        totals[2],
        totals[3],
        totals[4],
        totals[5],
    )


def solution(mesh):
    placed = (
        P("fsdp", "seq", None),
        P("fsdp", None),
        P("fsdp", None),
        P("fsdp", None),
        P("fsdp", None),
        P("fsdp"),
        P("fsdp"),
        P("fsdp"),
        P("fsdp", "seq", None),
    )
    return jax.shard_map(
        shards,
        mesh=mesh,
        in_specs=placed,
        out_specs=(
            P("fsdp", "seq", None),
            P("fsdp", "seq", None),
            P("fsdp", None),
            P("fsdp", None),
            P("fsdp", None),
            P("fsdp", None),
            P("fsdp"),
            P("fsdp"),
        ),
        check_vma=False,
    )
```

profile of v0, /device:TPU:0, one launch (start us, length us, event | category | flops | bytes accessed | tf_op | source)
XLA Modules:
  0.0 1163.0 jit_solution(13388341593110384322)
XLA Ops:
  11.6 15.9 %all-reduce.9 = (bf16[768]{0:T(1024)(128)(2,1)S(1)}, bf16[768]{0:T(1024)(128)(2,1)}) all-reduce(bf16[768]{0:T(1024)(128)(2,1)S(1)} %dynamic-update-slice, bf16[768]{0:T(1024)(128)(2,1)S(1)} %dynamic-update-slice.1), channel_id=1, replica_groups=mesh['seq'=4,'fsdp'=8] {'fsdp'}, use_global_device_ids=true, to_apply=%add.2 | all-reduce | flops 1536 | bytes 6144
  30.7 15.9 %all-gather.5.cloned.1.call-done = bf16[768,2304]{1,0:T(8,128)(2,1)} async-done(((bf16[96,2304]{1,0:T(8,128)(2,1)}), bf16[768,2304]{1,0:T(8,128)(2,1)}) %all-gather.5.cloned.1.call-update) | async-done | bytes 3538960 | tf_op jit(solution)/shard_map/all_gather | solution.py:62
  66.9 78.0 %all-to-all-done = bf16[768,3,4,192]{0,3,1,2:T(8,128)(2,1)S(1)} async-done(((bf16[768,3,4,192]{0,3,1,2:T(8,128)(2,1)}), bf16[768,3,4,192]{0,3,1,2:T(8,128)(2,1)S(1)}, u32[]{:S(2)}, u32[]{:S(2)}) %all-to-all-start) | async-done | bytes 3538976 | tf_op jit(solution)/shard_map/all_to_all | solution.py:85
  163.8 189.5 %while.28 = (s32[]{:T(128)}, bf16[6,512,3,64]{1,3,2,0:T(8,128)(2,1)}, f32[6,3,512]{2,1,0:T(4,128)}, bf16[6,512,3,64]{1,3,2,0:T(8,128)(2,1)S(1)}, bf16[3072,3,64]...) while((s32[]{:T(128)}, bf16[6,512,3,64]{1,3,2,0:T(8,128)(2,1)}, ...), condition=%wide.region_5.6_spmd.clone, body=%wide.region_2.5_spmd.clone.sunk | while | flops 1264682496 | bytes 59465864 | solution.py:111
  172.5 11.0 fusion.141
  183.4 11.3 fusion.142
  204.0 11.0 fusion.141
  215.0 11.3 fusion.142
  235.6 11.0 fusion.141
  246.6 11.3 fusion.142
  267.2 11.0 fusion.141
  278.2 11.3 fusion.142
  298.8 11.0 fusion.141
  309.7 11.3 fusion.142
  330.3 11.0 fusion.141
  341.3 11.3 fusion.142
  359.0 13.0 %reshape.302 = bf16[3072,1,192]{2,1,0:T(2,128)(2,1)} reshape(bf16[6,512,3,64]{3,2,1,0:T(4,128)(2,1)} %copy.131) | data formatting | bytes 2359296 | tf_op jit(solution)/shard_map/reshape | solution.py:112
  372.5 18.3 %reduce.1 = bf16[3072,192]{1,0:T(8,128)(2,1)S(1)} reduce(bf16[3072,1,192]{2,1,0:T(2,128)(2,1)} %reshape.302, bf16[]{:T(256)} %broadcast.245), dimensions={1}, to_apply=%reshape.302.reduce_sub_computation | reduce | bytes 2359298 | tf_op jit(solution)/shard_map/reshape | solution.py:112
  399.5 25.8 %all-to-all-done.1 = bf16[4,2,73728]{2,1,0:T(2,128)(2,1)S(1)} async-done(((bf16[4,2,73728]{2,1,0:T(2,128)(2,1)}), bf16[4,2,73728]{2,1,0:T(2,128)(2,1)S(1)}, u32[]{:S(2)}, u32[]{:S(2)}) %all-to-all-start.1) | async-done | bytes 1179680 | tf_op jit(solution)/shard_map/all_to_all | solution.py:113
  446.5 8.7 fusion.88
  455.2 13.3 %add_convert_fusion = (bf16[768,1152]{1,0:T(8,128)(2,1)}, f32[768,1152]{1,0:T(8,128)}, f32[768,1152]{1,0:T(8,128)}) fusion(f32[768,2304]{1,0:T(8,128)} %fusion.88, bf16[1152,768]{1,0:T(8,128)(2,1)} %all-gather.11.cloned.1.call-done, bf16[1,768,768]{2,1,0:T(8,128)(2,1)S(1)} %copy-done.20), kind=kOutput, calls=%fused_computation.62 | convolution fusion | flops 1423540224 | bytes 18874368 | tf_op jit(solution)/shard_map/dot_general | solution.py:47
  500.5 8.7 fusion.68
  509.2 19.3 %all-to-all-done.2 = bf16[768,4,192]{0,2,1:T(8,128)(2,1)} async-done(((bf16[768,4,192]{0,2,1:T(8,128)(2,1)}), bf16[768,4,192]{0,2,1:T(8,128)(2,1)}, u32[]{:S(2)}, u32[]{:S(2)}) %all-to-all-start.2) | async-done | bytes 1179680 | tf_op jit(solution)/shard_map/all_to_all | solution.py:145
  538.3 256.2 %while.29 = (s32[]{:T(128)}, f32[3072,3,64]{0,2,1:T(8,128)S(1)}, f32[3072,3,64]{0,2,1:T(8,128)}, bf16[6,512,3,64]{1,3,2,0:T(8,128)(2,1)}, bf16[6,512,3,64]{1,3,2...) while((s32[]{:T(128)}, f32[3072,3,64]{0,2,1:T(8,128)S(1)}, ...), condition=%wide.region_12.13_spmd.clone, body=%wide.region_10.12_spmd.clone.sunk | while | flops 3107882496 | bytes 146331856 | solution.py:176
  544.3 10.9 fusion.152
  555.2 10.4 fusion.153
  565.6 9.0 fusion.155
  586.7 12.4 %fusion.152 = (f32[3,512]{1,0:T(4,128)S(1)}, f32[3,512,3072]{2,1,0:T(8,128)}) fusion(bf16[3,512,3072]{2,1,0:T(8,128)(2,1)S(1)} %convolution_convert_fusion.3, f32[3,512]{1,0:T(4,128)S(1)} %dynamic-slice_bitcast_fusion.2, pred[3072]{0:T(1024)(128)(4,1)S(1)} %iota_compare_fusion.5, bf16[3072,3,64]{0,2,1:T(8,128)(2,1)S(1)} %get-tuple-element.531, ...), kind=kOutput, calls=%fused_computation.21.clone.1 | convolution fusion | flops 632289792 | bytes 29703172 | tf_op jit(solution)/shard_map/while/body/eval_jaxpr/qhd,khd->hqk/dot_general | solution.py:97
  599.1 11.3 fusion.153
  610.5 8.9 fusion.155
  631.4 10.9 fusion.152
  642.3 10.4 fusion.153
  652.8 8.7 fusion.155
  673.6 10.9 fusion.152
  684.5 10.3 fusion.153
  694.8 8.7 fusion.155
  715.6 10.9 fusion.152
  726.5 10.3 fusion.153
  736.9 8.7 fusion.155
  757.7 10.9 fusion.152
  768.6 10.3 fusion.153
  778.9 8.7 fusion.155
  810.9 143.3 %all_to_all.54 = bf16[3072,3,1,192]{3,1,2,0:T(4,128)(2,1)} all-to-all(bf16[3072,3,1,192]{3,1,2,0:T(4,128)(2,1)} %copy.123), channel_id=1, replica_groups=mesh['seq'=4,'fsdp'=8] {'seq'}, dimensions={0} | all-to-all | bytes 7077888 | tf_op jit(solution)/shard_map/all_to_all | solution.py:182
  954.2 8.2 copy.124
  982.4 63.5 %reduce-scatter.5.cloned.1.call-done = f32[96,2304]{1,0:T(8,128)} async-done(((f32[768,2304]{1,0:T(8,128)}), f32[96,2304]{1,0:T(8,128)}) %reduce-scatter.5.cloned.1.call-update) | async-done | bytes 884752 | tf_op jit(solution)/shard_map/reduce_scatter | solution.py:192
  1062.9 14.3 %all-reduce.6 = (f32[768]{0:T(1024)}, f32[768]{0:T(1024)}) all-reduce(f32[768]{0:T(1024)} %get-tuple-element.293, f32[768]{0:T(1024)} %get-tuple-element.291), channel_id=6, replica_groups=mesh['seq'=4,'fsdp'=8] {'fsdp'}, use_global_device_ids=true, to_apply=%region_24.25.clone | all-reduce | flops 1536 | bytes 12288
  1086.7 12.9 %all-reduce.7 = (f32[96]{0:T(128)}, f32[96]{0:T(128)}) all-reduce(f32[96]{0:T(128)} %dynamic-slice.3, f32[96]{0:T(128)} %dynamic-slice.5), channel_id=1, replica_groups=mesh['seq'=4,'fsdp'=8] {'seq'}, use_global_device_ids=true, to_apply=%region_25.26 | all-reduce | flops 192 | bytes 1536 | tf_op jit(solution)/shard_map/psum | solution.py:199
  1099.6 51.0 %all-reduce.12.cloned.1.call-done = (f32[96,2304]{1,0:T(8,128)}, f32[96,768]{1,0:T(8,128)}, f32[96,2304]{1,0:T(8,128)}, f32[144,768]{1,0:T(8,128)}) async-done(((f32[96,2304]{1,0:T(8,128)}, f32[96,768]{1,0:T(8,128)}, f32[96,2304]{1,0:T(8,128)}, f32[144,768]{1,0:T(8,128)}), (f32[96,2304]{1,0:T(8,128)}, f32[96,768]{1,0:T(8,128)}, f32[96,2304]{1,0:T(8,128)}, ...) | async-done | bytes 2506768 | tf_op jit(solution)/shard_map/psum | solution.py:199
  (271 shorter events, 319.3 us)
Async XLA Ops:
  7.2 39.5 %all-gather.5.cloned.1.call-start = ((), (), s32[]{:S(2)}) async-start(), calls=%async_computation.8 | async-start | bytes 3981312 | tf_op jit(solution)/shard_map/all_gather | solution.py:62
  27.5 24.9 %copy-start.33 = (f32[768]{0:T(1024)}, f32[768]{0:T(1024)S(1)}, u32[]{:S(2)}) copy-start(f32[768]{0:T(1024)S(1)} %convert_element_type.115) | copy-start | bytes 9220
  29.1 23.3 %copy-start.1 = (bf16[1,768,768]{1,2,0:T(8,128)(2,1)}, bf16[1,768,768]{1,2,0:T(8,128)(2,1)S(1)}, u32[]{:S(2)}) copy-start(bf16[1,768,768]{1,2,0:T(8,128)(2,1)S(1)} %copy.106) | copy-start | bytes 3538948
  29.3 23.1 %copy-start.31 = (f32[768]{0:T(1024)}, f32[768]{0:T(1024)S(1)}, u32[]{:S(2)}) copy-start(f32[768]{0:T(1024)S(1)} %broadcast_multiply_fusion.1) | copy-start | bytes 9220
  30.3 22.1 %copy-start.35 = (f32[768]{0:T(1024)}, f32[768]{0:T(1024)S(1)}, u32[]{:S(2)}) copy-start(f32[768]{0:T(1024)S(1)} %fusion.84) | copy-start | bytes 9220
  30.7 27.0 %copy-start.24 = (f32[768,32]{0,1:T(8,128)}, f32[768,32]{0,1:T(8,128)S(1)}, u32[]{:S(2)}) copy-start(f32[768,32]{0,1:T(8,128)S(1)} %get-tuple-element.356) | copy-start | bytes 294916
  30.7 27.0 %copy-start.26 = (f32[768,32]{0,1:T(8,128)}, f32[768,32]{0,1:T(8,128)S(1)}, u32[]{:S(2)}) copy-start(f32[768,32]{0,1:T(8,128)S(1)} %get-tuple-element.357) | copy-start | bytes 294916
  60.8 84.1 %all-to-all-start = ((bf16[768,3,4,192]{0,3,1,2:T(8,128)(2,1)}), bf16[768,3,4,192]{0,3,1,2:T(8,128)(2,1)S(1)}, u32[]{:S(2)}, u32[]{:S(2)}) async-start(bf16[768,3,4,192]{0,3,1,2:T(8,128)(2,1)} %pad_maximum_fusion), calls=%async_computation | async-start | bytes 7077888 | tf_op jit(solution)/shard_map/all_to_all | solution.py:85
  65.4 376.5 %all-gather.7.cloned.1.call-start = ((), (), s32[]{:S(2)}) async-start(), calls=%async_computation.9 | async-start | bytes 1327104 | tf_op jit(solution)/shard_map/all_gather | solution.py:63
  66.2 380.3 %all-gather.9.cloned.1.call-start = ((), (), s32[]{:S(2)}) async-start(), calls=%async_computation.10 | async-start | bytes 3981312 | tf_op jit(solution)/shard_map/all_gather | solution.py:64
  183.4 11.3 copy-start.29
  215.0 11.3 copy-start.29
  246.6 11.3 copy-start.29
  278.2 11.3 copy-start.29
  309.7 11.3 copy-start.29
  341.3 11.3 copy-start.29
  353.2 18.8 %copy-start = (bf16[3072,3,64]{0,2,1:T(8,128)(2,1)}, bf16[3072,3,64]{0,2,1:T(8,128)(2,1)S(1)}, u32[]{:S(2)}) copy-start(bf16[3072,3,64]{0,2,1:T(8,128)(2,1)S(1)} %get-tuple-element.563) | copy-start | bytes 3538948
  353.2 18.8 %copy-start.12 = (bf16[6,512,3,64]{1,3,2,0:T(8,128)(2,1)}, bf16[6,512,3,64]{1,3,2,0:T(8,128)(2,1)S(1)}, u32[]{:S(2)}) copy-start(bf16[6,512,3,64]{1,3,2,0:T(8,128)(2,1)S(1)} %get-tuple-element.567) | copy-start | bytes 3538948
  390.8 7.0 copy-start.40
  393.7 31.6 %all-to-all-start.1 = ((bf16[4,2,73728]{2,1,0:T(2,128)(2,1)}), bf16[4,2,73728]{2,1,0:T(2,128)(2,1)S(1)}, u32[]{:S(2)}, u32[]{:S(2)}) async-start(bf16[4,2,73728]{2,1,0:T(2,128)(2,1)} %reshape.305), calls=%async_computation.1 | async-start | bytes 2359296 | tf_op jit(solution)/shard_map/all_to_all | solution.py:113
  397.2 58.0 %all-gather.11.cloned.1.call-start = ((), (), s32[]{:S(2)}) async-start(), calls=%async_computation.11 | async-start | bytes 1990656 | tf_op jit(solution)/shard_map/all_gather | solution.py:65
  397.8 584.5 %reduce-scatter.7.cloned.1.call-start = ((), (), s32[]{:S(2)}) async-start(), calls=%async_computation.13 | async-start | bytes 2654208 | tf_op jit(solution)/shard_map/reduce_scatter | solution.py:193
  399.5 81.7 %copy-start.10 = (bf16[1,768,768]{1,2,0:T(8,128)(2,1)}, bf16[1,768,768]{1,2,0:T(8,128)(2,1)S(1)}, u32[]{:S(2)}) copy-start(bf16[1,768,768]{1,2,0:T(8,128)(2,1)S(1)} %copy.118) | copy-start | bytes 3538948
  436.0 6.0 copy-start.2
  446.4 8.8 copy-start.20
  455.2 13.3 %copy-start.4 = (f32[768,2304]{1,0:T(8,128)S(1)}, f32[768,2304]{1,0:T(8,128)}, u32[]{:S(2)}) copy-start(f32[768,2304]{1,0:T(8,128)} %fusion.88) | copy-start | bytes 21233668
  468.5 6.1 copy-start.8
  468.5 6.1 copy-start.14
  486.2 496.2 %reduce-scatter.11.cloned.1.call-start = ((), (), s32[]{:S(2)}) async-start(), calls=%async_computation.15 | async-start | bytes 3981312 | tf_op jit(solution)/shard_map/reduce_scatter | solution.py:195
  496.1 32.4 %all-to-all-start.2 = ((bf16[768,4,192]{0,2,1:T(8,128)(2,1)}), bf16[768,4,192]{0,2,1:T(8,128)(2,1)}, u32[]{:S(2)}, u32[]{:S(2)}) async-start(bf16[768,4,192]{0,2,1:T(8,128)(2,1)} %bitcast.18), calls=%async_computation.2 | async-start | bytes 2359296 | tf_op jit(solution)/shard_map/all_to_all | solution.py:145
  500.4 482.0 %reduce-scatter.9.cloned.1.call-start = ((), (), s32[]{:S(2)}) async-start(), calls=%async_computation.14 | async-start | bytes 7962624 | tf_op jit(solution)/shard_map/reduce_scatter | solution.py:194
  509.2 536.7 %reduce-scatter.5.cloned.1.call-start = ((), (), s32[]{:S(2)}) async-start(), calls=%async_computation.12 | async-start | bytes 7962624 | tf_op jit(solution)/shard_map/reduce_scatter | solution.py:192
  555.2 10.4 copy-start.16
  574.6 3.7 copy-start.17
  599.1 11.3 copy-start.16
  642.3 10.5 copy-start.16
  661.5 3.7 copy-start.17
  684.5 10.4 copy-start.16
  703.5 3.7 copy-start.17
  726.5 10.4 copy-start.16
  745.6 3.7 copy-start.17
  768.6 10.4 copy-start.16
  981.5 64.5 %copy-start.9 = (f32[768,768]{0,1:T(8,128)S(1)}, f32[768,768]{0,1:T(8,128)}, u32[]{:S(2)}) copy-start(f32[768,768]{0,1:T(8,128)} %copy-done.7) | copy-start | bytes 7077892
  981.5 169.2 %all-reduce.12.cloned.1.call-start = ((), (), s32[]{:S(2)}) async-start(), calls=%async_computation.16 | async-start | bytes 5013504 | tf_op jit(solution)/shard_map/psum | solution.py:199
  1053.3 6.5 copy-start.38
  1059.8 20.6 %copy-start.6 = (f32[768,768]{0,1:T(8,128)S(1)}, f32[768,768]{0,1:T(8,128)}, u32[]{:S(2)}) copy-start(f32[768,768]{0,1:T(8,128)} %copy-done.5) | copy-start | bytes 7077892
  1150.7 3.9 copy-start.28
  1150.7 4.9 copy-start.30
  (21 other events, 37.9 us)
Sparse Core Ops, SparseCore 0:
  9.9 36.7 all-gather.4
  68.1 24.5 all-gather.6
  94.6 33.9 all-gather.8
  399.6 26.9 all-gather.10
  486.3 40.6 reduce-scatter.6
  530.7 48.1 reduce-scatter.10
  582.8 65.4 reduce-scatter.8
  981.6 64.2 reduce-scatter.4
  1048.8 101.8 all-reduce.11
where the time goes:
time: 1170 us; the launch traced here: 1160 us
  matrix products  370 us (32%)
  waiting for transfers between devices  256 us (22%)
  blocking collectives  186 us (16%)
  other arithmetic  179 us (15%)
  local copies, waits for them, and re-layouts  142 us (12%)
  between operations  16.1 us (1%)
  starting transfers between devices  12.7 us (1%)
    all_to_all x1, blocking collectives, shards(): lax.all_to_all(grad_stack, 'seq', split_axis=0, concat_axis=2, tiled=True)  143 us
    dot_general x12, matrix products, scores(): jnp.einsum('qhd,khd->hqk', query_block, key_all, preferred_element_type=j...  115 us
    all_to_all x1, waiting for transfers between devices, shards(): lax.all_to_all(packed, 'seq', split_axis=2, concat_axis=0, tiled=True)  78 us
    dot_general x6, matrix products, attend(): jnp.einsum('hqk,khd->qhd', prob, value, preferred_element_type=jnp.float32)  67.9 us
    reduce_sum x6, other arithmetic, attend(): total = jnp.sum(expo, -1, keepdims=True)  65.8 us
    reduce_scatter x1, waiting for transfers between devices, shards(): lax.psum_scatter(grad_wqkv, 'fsdp', scatter_dimension=0, tiled=True)  63.5 us
    convert_element_type x6, other arithmetic, revisit(): grad_score = (prob * (grad_prob - weighted)).astype(jnp.bfloat16)  63.2 us
    dot_general x6, matrix products, revisit(): jnp.einsum('hqk,qhd->khd', prob_low, grad_block, preferred_element_type=j...  52.7 us
  transfers between devices with their start and end apart: 12, of which 6 were waited for; matrix products, arithmetic and copies ran while one was open for 54% of the time, Pallas kernels for 0%

commit v1 on v0

v1 whole, which is shorter than its diff:
```python
import functools
import math

import jax
import jax.numpy as jnp
from jax import lax
from jax.experimental import pallas as pl
from jax.experimental.pallas import tpu as pltpu
from jax.sharding import PartitionSpec as P

HEADS = 12


norm_eps = 1e-05
rope_base = 160000.0
masked_score = -1e30
LANES = 128
EVERY = ("zp", "zi", "chip", "core")
VMEM = 56 << 20


def dot(left, right, left_dim=1, right_dim=0):
    return lax.dot_general(
        left,
        right,
        (((left_dim,), (right_dim,)), ((), ())),
        preferred_element_type=jnp.float32,
    )


def call(kernel, grid, in_specs, out_specs, out_shape, scratch, flops, moved, exps=0):
    return pl.pallas_call(
        kernel,
        grid=grid,
        in_specs=in_specs,
        out_specs=out_specs,
        out_shape=out_shape,
        scratch_shapes=scratch,
        cost_estimate=pl.CostEstimate(flops=flops, bytes_accessed=moved, transcendentals=exps),
        compiler_params=pltpu.CompilerParams(vmem_limit_bytes=VMEM),
    )


def shape(dims, dtype):
    return jax.ShapeDtypeStruct(dims, dtype)


def rotary_tables(positions, half_dim):
    counter = jnp.arange(half_dim).astype(jnp.float32)
    inverse = jnp.exp(counter * (-math.log(rope_base) / half_dim))
    angles = positions[:, None] * inverse[None, :]
    cosine, sine = jnp.cos(angles), jnp.sin(angles)
    return (
        jnp.concatenate([cosine] * 4, -1),
        jnp.concatenate([-sine, sine, -sine, sine], -1),
    )


def swap_halves(values, head_dim):
    half = head_dim // 2
    lane = lax.broadcasted_iota(jnp.int32, values.shape, 1)
    ahead = pltpu.roll(values, LANES - half, 1)
    behind = pltpu.roll(values, half, 1)
    return jnp.where(lane % head_dim < half, ahead, behind)


def project_kernel(tiles, head_dim, own, other, gain, weight, cosine, sine, h_out, q_out, *kv_out):
    step = pl.program_id(0)
    values = jnp.where(step < tiles, own[...], other[...]).astype(jnp.float32)
    centre = values - jnp.mean(values, -1, keepdims=True)
    spread = jnp.mean(centre * centre, -1, keepdims=True)
    hidden = (centre * lax.rsqrt(spread + norm_eps) * gain[...]).astype(jnp.bfloat16)
    h_out[...] = hidden
    joined = dot(hidden, weight[...])
    width = q_out.shape[1]
    cos, sin = cosine[...], sine[...]
    factor = head_dim ** (-0.5) * math.log2(math.e)
    for pair in range(width // LANES):
        at = pair * LANES
        query = joined[:, at : at + LANES]
        query = query * cos + swap_halves(query, head_dim) * sin
        q_out[:, at : at + LANES] = (query * factor).astype(jnp.bfloat16)
        key = joined[:, width + at : width + at + LANES]
        key = key * cos + swap_halves(key, head_dim) * sin
        kv_out[pair][:, :LANES] = key.astype(jnp.bfloat16)
        value = joined[:, 2 * width + at : 2 * width + at + LANES]
        kv_out[pair][:, LANES:] = value.astype(jnp.bfloat16)


def project(own, other, gain, weight, cosine, sine, head_dim):
    rows, depth = own.shape
    block = 256
    tiles = rows // block
    width = weight.shape[1] // 3
    pairs = width // LANES
    by_row = lambda step: (step, 0)
    whole = lambda step: (0, 0)
    return call(
        functools.partial(project_kernel, tiles, head_dim),
        (2 * tiles,),
        [
            pl.BlockSpec((block, depth), lambda step: (jnp.minimum(step, tiles - 1), 0)),
            pl.BlockSpec((block, depth), lambda step: (jnp.maximum(step - tiles, 0), 0)),
            pl.BlockSpec((1, depth), whole),
            pl.BlockSpec(weight.shape, whole),
            pl.BlockSpec((block, LANES), by_row),
            pl.BlockSpec((block, LANES), by_row),
        ],
        [pl.BlockSpec((block, depth), by_row), pl.BlockSpec((block, width), by_row)]
        + [pl.BlockSpec((block, 2 * LANES), by_row)] * pairs,
        [shape((2 * rows, depth), jnp.bfloat16), shape((2 * rows, width), jnp.bfloat16)]
        + [shape((2 * rows, 2 * LANES), jnp.bfloat16)] * pairs,
        [],
        2 * 2 * rows * depth * 3 * width,
        2 * rows * (2 * depth + 3 * width) * 2 + weight.size * 2,
    )(own, other, gain, weight, cosine, sine)


def attend_kernel(head_dim, sources, first, last, *refs):
    refs = list(refs)
    query = refs.pop(0)
    keys = [(refs.pop(0), refs.pop(0)) for _ in range(sources)]
    if not first:
        acc_in, max_in = refs.pop(0), refs.pop(0)
    if last:
        mixed, log_total = refs.pop(0), refs.pop(0)
    else:
        acc_out, max_out = refs.pop(0), refs.pop(0)
    key_of, value_of, bias_of = refs
    span = keys[0][0].shape[0]

    @pl.when(pl.program_id(0) == 0)
    def prepare():
        low = lax.broadcasted_iota(jnp.int32, (span, LANES), 1) < head_dim
        one = jnp.ones((span, LANES), jnp.bfloat16)
        zero = jnp.zeros((span, LANES), jnp.bfloat16)
        for source, (key_value, bias) in enumerate(keys):
            part = pl.ds(source * span, span)
            key, value = key_value[:, :LANES], key_value[:, LANES:]
            key_of[0, part, :] = jnp.where(low, key, zero)
            key_of[1, part, :] = jnp.where(low, zero, key)
            value_of[0, part, :] = jnp.where(low, value, one)
            value_of[1, part, :] = jnp.where(low, one, value)
            bias_of[:, part] = bias[...]

    low = lax.broadcasted_iota(jnp.int32, (query.shape[0], LANES), 1) < head_dim
    held = query[...]
    results, tops = [], []
    for head in range(2):
        score = dot(held, key_of[head], 1, 1) + bias_of[...]
        top = jnp.max(score, 1, keepdims=True)
        if not first:
            before = max_in[:, head * head_dim : head * head_dim + 1]
            top = jnp.maximum(top, before)
        expo = jnp.exp2(score - top).astype(jnp.bfloat16)
        result = dot(expo, value_of[head])
        if not first:
            result = result + acc_in[:, head * LANES : (head + 1) * LANES] * jnp.exp2(before - top)
        results.append(result)
        tops.append(top)
    top = jnp.where(low, tops[0], tops[1])
    if last:
        total = jnp.where(
            low, pltpu.roll(results[0], head_dim, 1), pltpu.roll(results[1], head_dim, 1)
        )
        mixed[...] = (jnp.where(low, results[0], results[1]) / total).astype(mixed.dtype)
        log_total[...] = top + jnp.log2(total)
    else:
        acc_out[:, :LANES] = results[0]
        acc_out[:, LANES:] = results[1]
        max_out[...] = top


def attend(query, pair, keys, state=None, last=True, head_dim=64):
    rows = query.shape[0]
    span = keys[0][0].shape[0]
    block = min(512, rows)
    by_row = lambda step: (step, 0)
    whole = lambda step: (0, 0)
    narrow = pl.BlockSpec((block, LANES), by_row)
    wide = pl.BlockSpec((block, 2 * LANES), by_row)
    in_specs = [pl.BlockSpec((block, LANES), lambda step: (step, pair))]
    args = [query]
    for key_value, bias in keys:
        in_specs += [pl.BlockSpec((span, 2 * LANES), whole), pl.BlockSpec((1, span), whole)]
        args += [key_value, bias]
    if state is not None:
        in_specs += [wide, narrow]
        args += list(state)
    if last:
        out_specs = [narrow, narrow]
        out_shape = [shape((rows, LANES), jnp.bfloat16), shape((rows, LANES), jnp.float32)]
    else:
        out_specs = [wide, narrow]
        out_shape = [shape((rows, 2 * LANES), jnp.float32), shape((rows, LANES), jnp.float32)]
    count = span * len(keys)
    return call(
        functools.partial(attend_kernel, head_dim, len(keys), state is None, last),
        (rows // block,),
        in_specs,
        out_specs,
        out_shape,
        [
            pltpu.VMEM((2, count, LANES), jnp.bfloat16),
            pltpu.VMEM((2, count, LANES), jnp.bfloat16),
            pltpu.VMEM((1, count), jnp.float32),
        ],
        2 * 2 * 2 * rows * count * 256,
        rows * LANES * 8 + count * 512,
        2 * rows * count,
    )(*args)


def revisit_kernel(
    head_dim, key_value, bias, query, mixed, grad, log_total, dq_out, dkv_out,
    grad_key, grad_value, key_of, value_of,
):
    span = key_value.shape[0]
    step = pl.program_id(0)

    @pl.when(step == 0)
    def prepare():
        low = lax.broadcasted_iota(jnp.int32, (span, LANES), 1) < head_dim
        zero = jnp.zeros((span, LANES), jnp.bfloat16)
        key, value = key_value[:, :LANES], key_value[:, LANES:]
        key_of[0] = jnp.where(low, key, zero)
        key_of[1] = jnp.where(low, zero, key)
        value_of[0] = jnp.where(low, value, zero)
        value_of[1] = jnp.where(low, zero, value)
        grad_key[...] = jnp.zeros_like(grad_key)
        grad_value[...] = jnp.zeros_like(grad_value)

    rows = query.shape[0]
    block = min(256, rows)
    for start in range(0, rows, block):
        part = pl.ds(start, block)
        held, back = query[part, :], grad[part, :]
        held_t, back_t = held.T, back.T
        product = back.astype(jnp.float32) * mixed[part, :].astype(jnp.float32)
        grad_query = None
        for head in range(2):
            lanes = slice(head * head_dim, (head + 1) * head_dim)
            weighted = jnp.sum(product[:, lanes], 1, keepdims=True)
            log_block = log_total[part, head * head_dim : head * head_dim + 1]
            prob = jnp.exp2(dot(held, key_of[head], 1, 1) + bias[...] - log_block)
            grad_prob = dot(back, value_of[head], 1, 1)
            grad_score = (prob * (grad_prob - weighted)).astype(jnp.bfloat16)
            grad_value[lanes, :] += dot(back_t[lanes], prob.astype(jnp.bfloat16))
            grad_key[lanes, :] += dot(held_t[lanes], grad_score)
            term = dot(grad_score, key_of[head])
            grad_query = term if grad_query is None else grad_query + term
        dq_out[part, :] = grad_query * head_dim ** (-0.5)

    @pl.when(step == pl.num_programs(0) - 1)
    def finish():
        dkv_out[:, :LANES] = (grad_key[...].T * math.log(2.0)).astype(dkv_out.dtype)
        dkv_out[:, LANES:] = grad_value[...].T.astype(dkv_out.dtype)


def revisit(query, pair, key_value, bias, mixed, grad, log_total, head_dim=64):
    rows = query.shape[0]
    span = key_value.shape[0]
    block = min(512, rows)
    by_row = lambda step: (step, 0)
    by_pair = lambda step: (step, pair)
    whole = lambda step: (0, 0)
    narrow = pl.BlockSpec((block, LANES), by_row)
    return call(
        functools.partial(revisit_kernel, head_dim),
        (rows // block,),
        [
            pl.BlockSpec((span, 2 * LANES), whole),
            pl.BlockSpec((1, span), whole),
            pl.BlockSpec((block, LANES), by_pair),
            narrow,
            pl.BlockSpec((block, LANES), by_pair),
            narrow,
        ],
        [narrow, pl.BlockSpec((span, 2 * LANES), whole)],
        [shape((rows, LANES), jnp.float32), shape((span, 2 * LANES), jnp.bfloat16)],
        [
            pltpu.VMEM((LANES, span), jnp.float32),
            pltpu.VMEM((LANES, span), jnp.float32),
            pltpu.VMEM((2, span, LANES), jnp.bfloat16),
            pltpu.VMEM((2, span, LANES), jnp.bfloat16),
        ],
        5 * 2 * 2 * rows * span * 200,
        rows * LANES * 14 + span * 1024,
        2 * rows * span,
    )(key_value, bias, query, mixed, grad, log_total)


def unproject_kernel(pairs, head_dim, *refs):
    refs = list(refs)
    hidden, weight, cosine, sine = refs[:4]
    refs = refs[4:]
    near_q, far_q = refs[:pairs], refs[pairs : 2 * pairs]
    near_kv, far_kv = refs[2 * pairs : 3 * pairs], refs[3 * pairs : 4 * pairs]
    dh_out, dw_out, joined, total = refs[4 * pairs :]
    step = pl.program_id(0)
    width = pairs * LANES
    cos, sin = cosine[...], sine[...]
    for pair in range(pairs):
        at = pair * LANES
        query = near_q[pair][...] + far_q[pair][...]
        query = query * cos - swap_halves(query, head_dim) * sin
        joined[:, at : at + LANES] = query.astype(jnp.bfloat16)
        both = near_kv[pair][...].astype(jnp.float32) + far_kv[pair][...].astype(jnp.float32)
        key, value = both[:, :LANES], both[:, LANES:]
        key = key * cos - swap_halves(key, head_dim) * sin
        joined[:, width + at : width + at + LANES] = key.astype(jnp.bfloat16)
        joined[:, 2 * width + at : 2 * width + at + LANES] = value.astype(jnp.bfloat16)
    dh_out[...] = dot(joined[...], weight[...], 1, 1).astype(dh_out.dtype)
    share = dot(hidden[...], joined[...], 0, 0)

    @pl.when(step == 0)
    def begin():
        total[...] = share

    @pl.when(step > 0)
    def add():
        total[...] += share

    @pl.when(step == pl.num_programs(0) - 1)
    def finish():
        dw_out[...] = total[...].astype(dw_out.dtype)


def unproject(hidden, weight, cosine, sine, near_q, far_q, near_kv, far_kv, head_dim):
    rows, depth = hidden.shape
    block = 256
    pairs = len(near_q)
    by_row = lambda step: (step, 0)
    whole = lambda step: (0, 0)
    narrow = pl.BlockSpec((block, LANES), by_row)
    wide = pl.BlockSpec((block, 2 * LANES), by_row)
    return call(
        functools.partial(unproject_kernel, pairs, head_dim),
        (rows // block,),
        [pl.BlockSpec((block, depth), by_row), pl.BlockSpec(weight.shape, whole), narrow, narrow]
        + [narrow] * (2 * pairs)
        + [wide] * (2 * pairs),
        [pl.BlockSpec((block, depth), by_row), pl.BlockSpec(weight.shape, whole)],
        [shape((rows, depth), jnp.bfloat16), shape(weight.shape, jnp.bfloat16)],
        [pltpu.VMEM((block, weight.shape[1]), jnp.bfloat16), pltpu.VMEM(weight.shape, jnp.float32)],
        4 * rows * weight.size,
        rows * (depth * 4 + pairs * LANES * 16) + weight.size * 4,
    )(hidden, weight, cosine, sine, *near_q, *far_q, *near_kv, *far_kv)


def position(axes):
    place = 0
    for axis in axes:
        place = place * lax.axis_size(axis) + lax.axis_index(axis)
    return place


def others(axes):
    count = math.prod(lax.axis_size(axis) for axis in axes)
    return count, [
        [(source, source ^ step) for source in range(count)] for step in range(1, count)
    ]


def gather(block, axes):
    count, steps = others(axes)
    if count > 4:
        return lax.all_gather(block, axes, axis=0, tiled=True)
    place = position(axes)
    rows = block.shape[0]
    whole = jnp.zeros((count * rows,) + block.shape[1:], block.dtype)
    parts = [block] + [lax.ppermute(block, axes, pairs) for pairs in steps]
    for step, part in enumerate(parts):
        whole = lax.dynamic_update_slice_in_dim(whole, part, (place ^ step) * rows, 0)
    return whole


def scatter_sum(whole, axes):
    count, steps = others(axes)
    if count > 4:
        return lax.psum_scatter(whole, axes, scatter_dimension=0, tiled=True).astype(jnp.float32)
    place = position(axes)
    rows = whole.shape[0] // count
    total = lax.dynamic_slice_in_dim(whole, place * rows, rows, 0).astype(jnp.float32)
    for step, pairs in enumerate(steps, 1):
        block = lax.dynamic_slice_in_dim(whole, (place ^ step) * rows, rows, 0)
        total = total + lax.ppermute(block, axes, pairs).astype(jnp.float32)
    return total


def full_sum(values, axes):
    count, steps = others(axes)
    if count > 4:
        return lax.psum(values, axes)
    return values + sum(lax.ppermute(values, axes, pairs) for pairs in steps)


def core_swap(block):
    return lax.ppermute(block, "core", [(0, 1), (1, 0)])


def normalize(values, gain):
    centre = values - jnp.mean(values, -1, keepdims=True)
    spread = jnp.mean(centre * centre, -1, keepdims=True)
    return centre * lax.rsqrt(spread + norm_eps) * gain


def geglu(gate, upper):
    return jax.nn.gelu(gate, approximate=False) * upper


def shards(tokens, w_qkv, w_out, w_in, w_down, gain_attn, gain_mlp, lengths, cotangent):
    rows, width = tokens.shape[1:]
    head_dim = width // HEADS
    half = width // 2
    pairs = half // LANES
    chips = lax.axis_size("chip")
    core, inner = lax.axis_index("core"), lax.axis_index("zi")
    first_core = core == 0
    seq_axes = ("zp", "zi")
    low = jnp.bfloat16

    places = [(zp, zi, chip, c) for zp in range(2) for zi in range(2) for chip in range(chips) for c in range(2)]
    number = {place: index for index, place in enumerate(places)}
    move = [(number[(zp, zi, chip, c)], number[(c, zi, chip, zp)]) for zp, zi, chip, c in places]
    own = lax.ppermute(tokens[0], EVERY, move)
    length = lax.ppermute(lengths, EVERY, move)[0]
    grad_out = lax.ppermute(cotangent[0], EVERY, move)
    other = core_swap(own)

    shard = w_qkv.shape[0]
    by_core = w_qkv.reshape(shard, 3, 2, half)
    kept = jnp.where(first_core, by_core[:, :, 0], by_core[:, :, 1]).reshape(shard, 3 * half)
    given = jnp.where(first_core, by_core[:, :, 1], by_core[:, :, 0]).reshape(shard, 3 * half)
    taken = core_swap(given)
    weight = jnp.where(
        first_core, jnp.concatenate([kept, taken], 0), jnp.concatenate([taken, kept], 0)
    )
    weight = gather(weight, ("chip",))
    gains = jnp.stack([gain_attn, gain_mlp], 1)
    gains = jnp.concatenate([gains, core_swap(gains)], 0)
    gains = jnp.where(first_core, gains, jnp.roll(gains, shard, 0))
    gains = gather(gains, ("chip",)).astype(jnp.float32)
    first_gain, second_gain = gains[:, 0], gains[:, 1]

    m_out = lax.all_gather(w_out, ("chip", "core"), axis=0, tiled=True)
    m_in = lax.all_gather(w_in, ("chip", "core"), axis=0, tiled=True)
    m_down = lax.all_gather(w_down, ("chip", "core"), axis=0, tiled=True)

    steps = jnp.arange(rows)
    own_at = (2 * core + inner) * rows + steps
    other_at = (2 * (1 - core) + inner) * rows + steps
    here = jnp.concatenate([own_at, other_at])
    there = here + jnp.where(inner == 0, rows, -rows)
    cosine, sine = rotary_tables(here.astype(jnp.float32), head_dim // 2)
    near_bias = jnp.where(here < length, 0.0, masked_score).astype(jnp.float32)[None]
    far_bias = jnp.where(there < length, 0.0, masked_score).astype(jnp.float32)[None]

    hidden, query, *near = project(
        own, other, first_gain[None], weight, cosine, sine, head_dim
    )
    swap_chips = [(0, 1), (1, 0)]
    far = [lax.ppermute(key_value, "zi", swap_chips) for key_value in near]
    state = attend(query, pairs - 1, [(near[-1], near_bias)], last=False)
    attended = [
        attend(query, pair, [(near[pair], near_bias), (far[pair], far_bias)])
        for pair in range(pairs - 1)
    ]
    attended.append(attend(query, pairs - 1, [(far[-1], far_bias)], state))

    mine = jnp.concatenate([mixed[:rows] for mixed, _ in attended], 1)
    theirs = core_swap(jnp.concatenate([mixed[rows:] for mixed, _ in attended], 1))
    mixed = jnp.where(
        first_core, jnp.concatenate([mine, theirs], 1), jnp.concatenate([theirs, mine], 1)
    )

    inputs = own.astype(jnp.float32)
    resid = inputs + dot(mixed, m_out)
    h_second, second_norm_back = jax.vjp(normalize, resid, second_gain)
    h_second_low = h_second.astype(low)
    gate_up = dot(h_second_low, m_in)
    width_ff = gate_up.shape[1] // 2
    act, act_back = jax.vjp(geglu, gate_up[:, :width_ff], gate_up[:, width_ff:])
    act_low = act.astype(low)
    layer_out = (resid + dot(act_low, m_down)).astype(low)

    grad_down = dot(act_low, grad_out, 0, 0).astype(low)
    grad_act = dot(grad_out, m_down, 1, 1)
    grad_gate, grad_upper = act_back(grad_act)
    grad_gate_up = jnp.concatenate([grad_gate, grad_upper], 1).astype(low)
    grad_in = dot(h_second_low, grad_gate_up, 0, 0).astype(low)
    grad_h_second = dot(grad_gate_up, m_in, 1, 1)
    grad_resid_norm, grad_second_gain = second_norm_back(grad_h_second)
    grad_resid = grad_out.astype(jnp.float32) + grad_resid_norm
    grad_attn = grad_resid.astype(low)
    grad_wout = dot(mixed, grad_attn, 0, 0).astype(low)
    grad_mixed = dot(grad_attn, m_out, 1, 1).astype(low)

    kept = jnp.where(first_core, grad_mixed[:, :half], grad_mixed[:, half:])
    given = jnp.where(first_core, grad_mixed[:, half:], grad_mixed[:, :half])
    back = jnp.concatenate([kept, core_swap(given)], 0)

    far_grads = [
        revisit(query, pair, far[pair], far_bias, attended[pair][0], back, attended[pair][1])
        for pair in range(pairs)
    ]
    returned = [lax.ppermute(grads[1], "zi", swap_chips) for grads in far_grads]
    near_grads = [
        revisit(query, pair, near[pair], near_bias, attended[pair][0], back, attended[pair][1])
        for pair in range(pairs)
    ]
    grad_hidden, grad_weight = unproject(
        hidden,
        weight,
        cosine,
        sine,
        [grads[0] for grads in near_grads],
        [grads[0] for grads in far_grads],
        [grads[1] for grads in near_grads],
        returned,
        head_dim,
    )

    grad_h_first = grad_hidden[:rows].astype(jnp.float32) + core_swap(grad_hidden[rows:]).astype(
        jnp.float32
    )
    _, first_norm_back = jax.vjp(normalize, inputs, first_gain)
    grad_input_norm, grad_first_gain = first_norm_back(grad_h_first)
    grad_tokens = (grad_resid + grad_input_norm).astype(low)

    total = scatter_sum(grad_weight, ("chip",)).astype(low)
    total = gather(scatter_sum(total, seq_axes), seq_axes)
    kept = jnp.where(first_core, total[:shard], total[shard:])
    given = jnp.where(first_core, total[shard:], total[:shard])
    taken = core_swap(given)
    total_qkv = jnp.where(
        first_core, jnp.stack([kept, taken], 1), jnp.stack([taken, kept], 1)
    ).reshape(shard, 2, 3, half)
    total_qkv = total_qkv.transpose(0, 2, 1, 3).reshape(shard, 3 * width)

    shares = [
        lax.psum_scatter(grad, ("chip", "core"), scatter_dimension=0, tiled=True)
        for grad in (grad_wout, grad_in, grad_down)
    ]
    sums = lax.psum(tuple(shares), seq_axes)
    sums = [value.astype(jnp.float32) for value in sums]

    gain_sums = jnp.stack([grad_first_gain, grad_second_gain])
    gain_sums = gain_sums + core_swap(gain_sums)
    gain_sums = full_sum(full_sum(gain_sums, ("chip",)), seq_axes)
    place = position(("chip", "core"))
    gain_sums = lax.dynamic_slice_in_dim(gain_sums, place * shard, shard, 1)

    return (
        lax.ppermute(layer_out, EVERY, move)[None],
        lax.ppermute(grad_tokens, EVERY, move)[None],
        total_qkv,
        sums[0],
        sums[1],
        sums[2],
        gain_sums[0],
        gain_sums[1],
    )


def solution(mesh):
    devices = mesh.devices
    split = jax.sharding.Mesh(
        devices.reshape(2, devices.shape[0] // 2, devices.shape[1] // 2, 2), EVERY
    )
    seq, fsdp = ("zp", "zi"), ("chip", "core")
    activation, matrix, vector = P(fsdp, seq, None), P(fsdp, None), P(fsdp)
    return jax.shard_map(
        shards,
        mesh=split,
        in_specs=(activation, matrix, matrix, matrix, matrix, vector, vector, vector, activation),
        out_specs=(activation, activation, matrix, matrix, matrix, matrix, vector, vector),
        check_vma=False,
    )
```

time: 1170 us -> 547 us (0.47)
  matrix products: 370 us -> 49.8 us
  Pallas kernels: 0 us -> 186 us
  blocking collectives: 186 us -> 0 us
  other arithmetic: 179 us -> 34.6 us
  waiting for transfers between devices: 256 us -> 133 us
  local copies, waits for them, and re-layouts: 142 us -> 24.4 us
  starting transfers between devices: 12.7 us -> 96.9 us
    dot_general x54 -> x9, matrix products: 370 us -> 49.8 us  [dot(): lax.dot_general(left, right, (((left_dim,), (right_dim,)), ((), ())), pre...]
    pallas_call x0 -> x12, Pallas kernels: none -> 186 us  [the longest x6 94.5 us: revisit(): call(functools.partial(revisit_kernel, head_dim), (rows // block,), [pl.B...]
    all_to_all x1 -> x0, blocking collectives: 143 us -> none  [shards(): lax.all_to_all(grad_stack, 'seq', split_axis=0, concat_axis=2, tiled=True)]
    all_to_all x3 -> x0, waiting for transfers between devices: 123 us -> none  [the longest x1 78 us: shards(): lax.all_to_all(packed, 'seq', split_axis=2, concat_axis=0, tiled=True)]
    ppermute x0 -> x40, waiting for transfers between devices: none -> 120 us  [the longest x9 55.3 us: gather(): parts = [block] + [lax.ppermute(block, axes, pairs) for pairs in steps]]
    ppermute x0 -> x40, starting transfers between devices: none -> 96.5 us  [the longest x8 34.3 us: core_swap(): return lax.ppermute(block, 'core', [(0, 1), (1, 0)])]
    reduce_sum x6 -> x0, other arithmetic: 65.8 us -> none  [attend(): total = jnp.sum(expo, -1, keepdims=True)]
    reduce_scatter x4 -> x3, waiting for transfers between devices: 63.6 us -> 0.01 us  [shards(): lax.psum_scatter(grad, ('chip', 'core'), scatter_dimension=0, tiled=True)]
  transfers between devices with their start and end apart: 12 -> 47, of which waited for: 6 -> 11; matrix products, arithmetic and copies ran while one was open for 54% -> 12% of each run, Pallas kernels for 0% -> 34%
where the time goes in v1:
time: 547 us; the launch traced here: 539 us
  Pallas kernels  186 us (34%)
  waiting for transfers between devices  133 us (24%)
  starting transfers between devices  96.9 us (18%)
  matrix products  49.8 us (9%)
  other arithmetic  34.6 us (6%)
  local copies, waits for them, and re-layouts  24.4 us (4%)
  between operations  15.1 us (3%)
    pallas_call x6, Pallas kernels, revisit(): call(functools.partial(revisit_kernel, head_dim), (rows // block,), [pl.B...  94.5 us
    pallas_call x4, Pallas kernels, attend(): call(functools.partial(attend_kernel, head_dim, len(keys), state is None,...  66.1 us
    ppermute x9, waiting for transfers between devices, gather(): parts = [block] + [lax.ppermute(block, axes, pairs) for pairs in steps]  55.3 us
    dot_general x9, matrix products, dot(): lax.dot_general(left, right, (((left_dim,), (right_dim,)), ((), ())), pre...  49.8 us
    ppermute x8, starting transfers between devices, core_swap(): return lax.ppermute(block, 'core', [(0, 1), (1, 0)])  34.3 us
    ppermute x6, waiting for transfers between devices, full_sum(): return values + sum((lax.ppermute(values, axes, pairs) for pairs in steps))  29.7 us
    ppermute x6, waiting for transfers between devices, scatter_sum(): total = total + lax.ppermute(block, axes, pairs).astype(jnp.float32)  25.1 us
    pallas_call x1, Pallas kernels, unproject(): call(functools.partial(unproject_kernel, pairs, head_dim), (rows // block...  15.8 us
  transfers between devices with their start and end apart: 47, of which 11 were waited for; matrix products, arithmetic and copies ran while one was open for 12% of the time, Pallas kernels for 34%

profile of v1, /device:TPU:0, one launch (start us, length us, event | category | flops | bytes accessed | tf_op | source)
XLA Modules:
  0.0 539.3 jit_solution(14752686456369494764)
XLA Ops:
  13.6 2.8 fusion.19
  16.4 2.4 pad_maximum_fusion.4
  19.9 2.9 collective-permute-start.7
  22.8 21.4 %collective-permute-start.1 = (bf16[768,768]{1,0:T(8,128)(2,1)S(1)}, bf16[768,768]{1,0:T(8,128)(2,1)}, u32[]{:S(2)}, u32[]{:S(2)}) collective-permute-start(bf16[768,768]{1,0:T(8,128)(2,1)S(1)} %collective-permute-done.own), channel_id=1, source_target_pairs={{0,1},{1,0},{2,3},{3,2},{4,5},{5,4},{6,7},{7,6},{8,9},{9,8},{10,11... | collective-permute-start | bytes 3538952 | tf_op jit(solution)/shard_map/ppermute | solution.py:399
  55.2 20.1 %collective-permute-done.8 = bf16[192,1152]{1,0:T(8,128)(2,1)S(1)} collective-permute-done((bf16[192,1152]{1,0:T(8,128)(2,1)}, bf16[192,1152]{1,0:T(8,128)(2,1)S(1)}, u32[]{:S(2)}, u32[]{:S(2)}) %collective-permute-start.8) | collective-permute-done | bytes 442400 | tf_op jit(solution)/shard_map/ppermute | solution.py:372
  76.6 9.2 %shard_map.152 = (bf16[1536,768]{1,0:T(8,128)(2,1)}, bf16[1536,384]{1,0:T(8,128)(2,1)}, bf16[1536,256]{1,0:T(8,128)(2,1)}, bf16[1536,256]{1,0:T(8,128)(2,1)}, bf16[1536,256]{1,0:T(8,128)(2,1)}) custom-call(bf16[768,768]{1,0:T(8,128)(2,1)} %copy-done, bf16[768,768]{1,0:T(8,128)(2,1)} %collective-permute-done.1.other, f32[1,768]{1,0:T(1,128)} %get-tuple-element.106.gain, ...), custom_call_target="tpu_custom_call" | custom-call | flops 2717908992 | bytes 10027008 | tf_op jit(solution)/shard_map/pallas_call | solution.py:98
  90.2 11.3 %shard_map.155 = (f32[1536,256]{1,0:T(8,128)}, f32[1536,128]{1,0:T(8,128)}) custom-call(bf16[1536,384]{1,0:T(8,128)(2,1)} %get-tuple-element.35.refs_0_.query, bf16[1536,256]{1,0:T(8,128)(2,1)} %get-tuple-element.40.refs_1_.key_value, f32[1,1536]{1,0:T(1,128)} %get-tuple-element.107.refs_2_.bias), custom_call_target="tpu_custom_call" | custom-call | flops 4831838208 | bytes 2359296 | tf_op jit(solution)/shard_map/pallas_call | solution.py:197
  101.5 5.1 collective-permute-done.11.refs_3_.key_value
  107.5 21.2 %shard_map.153 = (bf16[1536,128]{1,0:T(8,128)(2,1)}, f32[1536,128]{1,0:T(8,128)}) custom-call(bf16[1536,384]{1,0:T(8,128)(2,1)} %get-tuple-element.35.refs_0_.query, bf16[1536,256]{1,0:T(8,128)(2,1)} %get-tuple-element.36.refs_1_.key_value, f32[1,1536]{1,0:T(1,128)} %get-tuple-element.107.refs_2_.bias, bf16[1536,256]{1,0:T(8,128)(2,1)} %copy-done.24, ...), custom_call_target="tpu_custom_call" | custom-call | flops 9663676416 | bytes 3145728 | tf_op jit(solution)/shard_map/pallas_call | solution.py:197
  131.2 20.8 %shard_map.154 = (bf16[1536,128]{1,0:T(8,128)(2,1)}, f32[1536,128]{1,0:T(8,128)}) custom-call(bf16[1536,384]{1,0:T(8,128)(2,1)} %get-tuple-element.35.refs_0_.query, bf16[1536,256]{1,0:T(8,128)(2,1)} %get-tuple-element.38.refs_1_.key_value, f32[1,1536]{1,0:T(1,128)} %get-tuple-element.107.refs_2_.bias, bf16[1536,256]{1,0:T(8,128)(2,1)} %copy-done.25, ...), custom_call_target="tpu_custom_call" | custom-call | flops 9663676416 | bytes 3145728 | tf_op jit(solution)/shard_map/pallas_call | solution.py:197
  153.0 12.8 %shard_map.156 = (bf16[1536,128]{1,0:T(8,128)(2,1)}, f32[1536,128]{1,0:T(8,128)}) custom-call(bf16[1536,384]{1,0:T(8,128)(2,1)} %get-tuple-element.35.refs_0_.query, bf16[1536,256]{1,0:T(8,128)(2,1)} %copy-done.26, f32[1,1536]{1,0:T(1,128)} %get-tuple-element.108.refs_4_.refs_2_.bias, f32[1536,256]{1,0:T(8,128)} %get-tuple-element.41.refs_3_, ...), custom_call_target="tpu_custom_call" | custom-call | flops 4831838208 | bytes 2359296 | tf_op jit(solution)/shard_map/pallas_call | solution.py:197
  168.4 10.4 %collective-permute-start.16 = (bf16[768,768]{1,0:T(8,128)(2,1)}, bf16[768,768]{1,0:T(8,128)(2,1)}, u32[]{:S(2)}, u32[]{:S(2)}) collective-permute-start(bf16[768,768]{1,0:T(8,128)(2,1)} %bitcast.6), channel_id=1, source_target_pairs={{0,0},{1,16},{2,2},{3,18},{4,4},{5,20},{6,6},{7,22},{8,8},{9,24},{... | collective-permute-start | bytes 3538952 | tf_op jit(solution)/shard_map/ppermute | solution.py:428
  179.6 3.2 fusion.36
  183.3 7.6 %fusion.28 = f32[768,2304]{1,0:T(8,128)} fusion(bf16[768,2304]{1,0:T(8,128)(2,1)} %all-gather.6.cloned.1.call-done, f32[768,768]{1,0:T(8,128)S(1)} %get-tuple-element.114, f32[768]{0:T(1024)S(1)} %get-tuple-element.69, f32[768]{0:T(1024)S(1)} %fusion.20, f32[768]{0:T(1024)S(1)} %broadcast_multiply_fusion.1), kind=kOutput, calls=%fused_computation.119 | convolution fusion | flops 2720268288 | bytes 12985344 | tf_op jit(solution)/shard_map/dot_general | solution.py:23
  190.9 13.4 %add_convert_fusion = (bf16[768,1152]{1,0:T(8,128)(2,1)}, f32[768,1152]{1,0:T(8,128)S(1)}, f32[768,1152]{1,0:T(8,128)S(1)}) fusion(f32[768,2304]{1,0:T(8,128)} %fusion.28, bf16[768,768]{1,0:T(8,128)(2,1)} %collective-permute-done.16, bf16[1152,768]{1,0:T(8,128)(2,1)} %all-gather.8.cloned.1.call-done), kind=kOutput, calls=%fused_computation.5 | convolution fusion | flops 1423540224 | bytes 18874368 | tf_op jit(solution)/shard_map/dot_general | solution.py:23
  204.2 2.7 multiply_convert_fusion
  206.9 6.7 %multiply_reduce_fusion = (f32[768]{0:T(1024)}, f32[768]{0:T(1024)S(1)}, f32[768,768]{1,0:T(8,128)S(1)}) fusion(f32[768,768]{1,0:T(8,128)S(1)} %get-tuple-element.114, f32[768]{0:T(1024)S(1)} %fusion.20, f32[768]{0:T(1024)S(1)} %broadcast_multiply_fusion.1, f32[768]{0:T(1024)S(1)} %get-tuple-element.69, bf16[768,2304]{1,0:T(8,128)(2,1)} %all-gather.6.cloned.1.call-done, ...), kind=kOutput, calls=%fused_computation.36 | convolution fusion | flops 2729114112 | bytes 11811840 | tf_op jit(solution)/shard_map/dot_general | solution.py:23
  213.7 2.5 fusion.30
  221.2 4.7 convolution_convert_fusion.1
  226.2 2.9 convolution_convert_fusion.3
  230.2 9.4 %collective-permute-start.17 = (bf16[768,384]{1,0:T(8,128)(2,1)}, bf16[768,384]{1,0:T(8,128)(2,1)}, u32[]{:S(2)}, u32[]{:S(2)}) collective-permute-start(bf16[768,384]{1,0:T(8,128)(2,1)} %get-tuple-element.87), channel_id=1, source_target_pairs={{0,1},{1,0},{2,3},{3,2},{4,5},{5,4},{6,7},{7,6},{8,9},{9,8},{10,11... | collective-permute-start | bytes 1769480 | tf_op jit(solution)/shard_map/ppermute | solution.py:399
  239.7 5.1 convolution_convert_fusion
  244.8 2.4 pad_maximum_fusion.3.grad
  247.2 15.6 %shard_map.159 = (f32[1536,128]{1,0:T(8,128)}, bf16[1536,256]{1,0:T(8,128)(2,1)}) custom-call(bf16[1536,256]{1,0:T(8,128)(2,1)} %get-tuple-element.40.refs_1_.key_value, f32[1,1536]{1,0:T(1,128)} %get-tuple-element.107.refs_2_.bias, bf16[1536,384]{1,0:T(8,128)(2,1)} %get-tuple-element.35.refs_0_.query, bf16[1536,128]{1,0:T(8,128)(2,1)} %get-tuple-element.43.mixed, ...), custom_call_target="tpu_custom_call" | custom-call | flops 9437184000 | bytes 4325376 | tf_op jit(solution)/shard_map/pallas_call | solution.py:268
  262.8 15.7 %shard_map.162 = (f32[1536,128]{1,0:T(8,128)}, bf16[1536,256]{1,0:T(8,128)(2,1)}) custom-call(bf16[1536,256]{1,0:T(8,128)(2,1)} %copy-done.26, f32[1,1536]{1,0:T(1,128)} %get-tuple-element.108.refs_4_.refs_2_.bias, bf16[1536,384]{1,0:T(8,128)(2,1)} %get-tuple-element.35.refs_0_.query, bf16[1536,128]{1,0:T(8,128)(2,1)} %get-tuple-element.43.mixed, ...), custom_call_target="tpu_custom_call" | custom-call | flops 9437184000 | bytes 4325376 | tf_op jit(solution)/shard_map/pallas_call | solution.py:268
  278.5 15.9 %shard_map.158 = (f32[1536,128]{1,0:T(8,128)}, bf16[1536,256]{1,0:T(8,128)(2,1)}) custom-call(bf16[1536,256]{1,0:T(8,128)(2,1)} %get-tuple-element.38.refs_1_.key_value, f32[1,1536]{1,0:T(1,128)} %get-tuple-element.107.refs_2_.bias, bf16[1536,384]{1,0:T(8,128)(2,1)} %get-tuple-element.35.refs_0_.query, bf16[1536,128]{1,0:T(8,128)(2,1)} %get-tuple-element.39.mixed, ...), custom_call_target="tpu_custom_call" | custom-call | flops 9437184000 | bytes 4325376 | tf_op jit(solution)/shard_map/pallas_call | solution.py:268
  294.4 15.6 %shard_map.161 = (f32[1536,128]{1,0:T(8,128)}, bf16[1536,256]{1,0:T(8,128)(2,1)}) custom-call(bf16[1536,256]{1,0:T(8,128)(2,1)} %copy-done.25, f32[1,1536]{1,0:T(1,128)} %get-tuple-element.108.refs_4_.refs_2_.bias, bf16[1536,384]{1,0:T(8,128)(2,1)} %get-tuple-element.35.refs_0_.query, bf16[1536,128]{1,0:T(8,128)(2,1)} %get-tuple-element.39.mixed, ...), custom_call_target="tpu_custom_call" | custom-call | flops 9437184000 | bytes 4325376 | tf_op jit(solution)/shard_map/pallas_call | solution.py:268
  312.1 16.0 %shard_map.160 = (f32[1536,128]{1,0:T(8,128)}, bf16[1536,256]{1,0:T(8,128)(2,1)}) custom-call(bf16[1536,256]{1,0:T(8,128)(2,1)} %copy-done.24, f32[1,1536]{1,0:T(1,128)} %get-tuple-element.108.refs_4_.refs_2_.bias, bf16[1536,384]{1,0:T(8,128)(2,1)} %get-tuple-element.35.refs_0_.query, bf16[1536,128]{1,0:T(8,128)(2,1)} %get-tuple-element.37.mixed, ...), custom_call_target="tpu_custom_call" | custom-call | flops 9437184000 | bytes 4325376 | tf_op jit(solution)/shard_map/pallas_call | solution.py:268
  328.1 15.6 %shard_map.157 = (f32[1536,128]{1,0:T(8,128)}, bf16[1536,256]{1,0:T(8,128)(2,1)}) custom-call(bf16[1536,256]{1,0:T(8,128)(2,1)} %get-tuple-element.36.refs_1_.key_value, f32[1,1536]{1,0:T(1,128)} %get-tuple-element.107.refs_2_.bias, bf16[1536,384]{1,0:T(8,128)(2,1)} %get-tuple-element.35.refs_0_.query, bf16[1536,128]{1,0:T(8,128)(2,1)} %get-tuple-element.37.mixed, ...), custom_call_target="tpu_custom_call" | custom-call | flops 9437184000 | bytes 4325376 | tf_op jit(solution)/shard_map/pallas_call | solution.py:268
  343.8 4.4 collective-permute-done.18.refs_13_
  349.1 15.8 %shard_map.163 = (bf16[1536,768]{1,0:T(8,128)(2,1)}, bf16[768,1152]{1,0:T(8,128)(2,1)}) custom-call(bf16[1536,768]{1,0:T(8,128)(2,1)} %get-tuple-element.44.refs_0_, bf16[768,1152]{1,0:T(8,128)(2,1)} %copy-done.10, f32[1536,128]{1,0:T(8,128)} %get-tuple-element.117.cosine.refs_2_, f32[1536,128]{1,0:T(8,128)} %get-tuple-element.118.sine.refs_3_, ...), custom_call_target="tpu_custom_call" | custom-call | flops 5435817984 | bytes 17694720 | tf_op jit(solution)/shard_map/pallas_call | solution.py:337
  364.9 2.4 constant_dynamic-slice_fusion.9
  371.0 9.7 %collective-permute-done.23 = bf16[192,1152]{1,0:T(8,128)(2,1)} collective-permute-done((bf16[192,1152]{1,0:T(8,128)(2,1)}, bf16[192,1152]{1,0:T(8,128)(2,1)}, u32[]{:S(2)}, u32[]{:S(2)}) %collective-permute-start.23) | collective-permute-done | bytes 442400 | tf_op jit(solution)/shard_map/ppermute | solution.py:387
  380.7 9.5 %collective-permute-done.24 = bf16[192,1152]{1,0:T(8,128)(2,1)} collective-permute-done((bf16[192,1152]{1,0:T(8,128)(2,1)}, bf16[192,1152]{1,0:T(8,128)(2,1)}, u32[]{:S(2)}, u32[]{:S(2)}) %collective-permute-start.24) | collective-permute-done | bytes 442400 | tf_op jit(solution)/shard_map/ppermute | solution.py:387
  393.2 3.1 collective-permute-start.28
  396.5 2.4 collective-permute-done.26
  398.9 3.6 collective-permute-done.27
  404.8 4.2 add_convert_fusion.2
  409.0 10.4 %collective-permute-start.15 = (bf16[768,768]{1,0:T(8,128)(2,1)}, bf16[768,768]{1,0:T(8,128)(2,1)}, u32[]{:S(2)}, u32[]{:S(2)}) collective-permute-start(bf16[768,768]{1,0:T(8,128)(2,1)} %add_convert_fusion.2), channel_id=1, source_target_pairs={{0,0},{1,16},{2,2},{3,18},{4,4},{5,20},{6,6},{7,22},{8,8},{9,24},{... | collective-permute-start | bytes 3538952 | tf_op jit(solution)/shard_map/ppermute | solution.py:555
  419.4 2.4 collective-permute-start.31
  421.8 34.0 %collective-permute-done.30 = f32[48,1152]{1,0:T(8,128)S(1)} collective-permute-done((f32[48,1152]{1,0:T(8,128)S(1)}, f32[48,1152]{1,0:T(8,128)S(1)}, u32[]{:S(2)}, u32[]{:S(2)}) %collective-permute-start.30) | collective-permute-done | bytes 221216 | tf_op jit(solution)/shard_map/ppermute | solution.py:372
  458.7 3.3 add_convert_fusion.1
  469.4 2.6 collective-permute-start.32
  472.0 2.8 collective-permute-start.37
  474.8 3.0 collective-permute-start.38
  478.2 29.7 %collective-permute-done.38 = f32[2,768]{1,0:T(2,128)S(1)} collective-permute-done((f32[2,768]{1,0:T(2,128)S(1)}, f32[2,768]{1,0:T(2,128)S(1)}, u32[]{:S(2)}, u32[]{:S(2)}) %collective-permute-start.38) | collective-permute-done | bytes 6176 | tf_op jit(solution)/shard_map/ppermute | solution.py:395
  511.9 11.7 %all-reduce.3.cloned.1.call-done = (bf16[96,768]{1,0:T(8,128)(2,1)}, bf16[96,2304]{1,0:T(8,128)(2,1)}, bf16[144,768]{1,0:T(8,128)(2,1)}) async-done(((bf16[96,768]{1,0:T(8,128)(2,1)}, bf16[96,2304]{1,0:T(8,128)(2,1)}, bf16[144,768]{1,0:T(8,128)(2,1)}), (bf16[96,768]{1,0:T(8,128)(2,1)}, bf16[96,2304]{1,0:T(8,128)(2,1)}, bf16[144,768]{1,0:T(8,128)(2,1)})) %all-reduce.3.cloned.1.call-update) | async-done | bytes 811024 | tf_op jit(solution)/shard_map/psum | solution.py:545
  528.9 2.4 copy.61
  (215 shorter events, 71.5 us)
Async XLA Ops:
  7.2 171.6 %all-gather.4.cloned.1.call-start = ((), (), s32[]{:S(2)}) async-start(), calls=%async_computation.3 | async-start | bytes 1327104 | tf_op jit(solution)/shard_map/all_gather | solution.py:446
  7.9 175.4 %all-gather.6.cloned.1.call-start = ((), (), s32[]{:S(2)}) async-start(), calls=%async_computation.4 | async-start | bytes 3981312 | tf_op jit(solution)/shard_map/all_gather | solution.py:447
  8.7 182.2 %all-gather.8.cloned.1.call-start = ((), (), s32[]{:S(2)}) async-start(), calls=%async_computation.5 | async-start | bytes 1990656 | tf_op jit(solution)/shard_map/all_gather | solution.py:448
  10.8 8.0 %collective-permute-start.6 = (bf16[96,1152]{1,0:T(8,128)(2,1)S(1)}, bf16[96,1152]{1,0:T(8,128)(2,1)S(1)}, u32[]{:S(2)}, u32[]{:S(2)}) collective-permute-start(bf16[96,1152]{1,0:T(8,128)(2,1)S(1)} %bitcast.39), channel_id=1, source_target_pairs={{0,1},{1,0},{2,3},{3,2},{4,5},{5,4},{6,7},{7,6},{8,9},{9,8},{10,11... | collective-permute-start | bytes 663560 | tf_op jit(solution)/shard_map/ppermute | solution.py:399
  11.4 32.9 %collective-permute-start.2 = (bf16[96,2]{0,1:T(2,128)(2,1)S(1)}, bf16[96,2]{0,1:T(2,128)(2,1)S(1)}, u32[]{:S(2)}, u32[]{:S(2)}) collective-permute-start(bf16[96,2]{0,1:T(2,128)(2,1)S(1)} %pad_maximum_fusion.8), channel_id=1, source_target_pairs={{0,1},{1,0},{2,3},{3,2},{4,5},{5,4},{6,7},{7,6},{8,9},{9,8},{10,11... | collective-permute-start | bytes 1160 | tf_op jit(solution)/shard_map/ppermute | solution.py:399
  11.5 11.3 %collective-permute-start = (bf16[768,768]{1,0:T(8,128)(2,1)}, bf16[768,768]{1,0:T(8,128)(2,1)S(1)}, u32[]{:S(2)}, u32[]{:S(2)}) collective-permute-start(bf16[768,768]{1,0:T(8,128)(2,1)} %bitcast), channel_id=1, source_target_pairs={{0,0},{1,16},{2,2},{3,18},{4,4},{5,20},{6,6},{7,22},{8,8},{9,24},{... | collective-permute-start | bytes 3538952 | tf_op jit(solution)/shard_map/ppermute | solution.py:426
  13.4 454.7 %reduce-scatter.4.cloned.1.call-start = ((), (), s32[]{:S(2)}) async-start(), calls=%async_computation.6 | async-start | bytes 1327104 | tf_op jit(solution)/shard_map/reduce_scatter | solution.py:542
  19.9 35.3 %collective-permute-start.7 = (bf16[192,1152]{1,0:T(8,128)(2,1)}, bf16[192,1152]{1,0:T(8,128)(2,1)S(1)}, u32[]{:S(2)}, u32[]{:S(2)}) collective-permute-start(bf16[192,1152]{1,0:T(8,128)(2,1)} %get-tuple-element.80), channel_id=1, source_target_pairs={{0,2},{2,0},{4,6},{6,4},{1,3},{3,1},{5,7},{7,5},{8,10},{10,8},{12,... | collective-permute-start | bytes 1327112 | tf_op jit(solution)/shard_map/ppermute | solution.py:372
  22.8 52.6 %collective-permute-start.1 = (bf16[768,768]{1,0:T(8,128)(2,1)S(1)}, bf16[768,768]{1,0:T(8,128)(2,1)}, u32[]{:S(2)}, u32[]{:S(2)}) collective-permute-start(bf16[768,768]{1,0:T(8,128)(2,1)S(1)} %collective-permute-done.own), channel_id=1, source_target_pairs={{0,1},{1,0},{2,3},{3,2},{4,5},{5,4},{6,7},{7,6},{8,9},{9,8},{10,11... | collective-permute-start | bytes 3538952 | tf_op jit(solution)/shard_map/ppermute | solution.py:399
  44.4 3.6 collective-permute-start.3
  45.9 4.6 collective-permute-start.4
  47.4 4.5 collective-permute-start.5
  48.0 39.0 %collective-permute-start.10 = (s32[1]{0:T(128)}, s32[1]{0:T(128)}, u32[]{:S(2)}, u32[]{:S(2)}) collective-permute-start(s32[1]{0:T(128)} %param.16), channel_id=1, source_target_pairs={{0,0},{1,16},{2,2},{3,18},{4,4},{5,20},{6,6},{7,22},{8,8},{9,24},{... | collective-permute-start | bytes 20 | tf_op jit(solution)/shard_map/ppermute | solution.py:427
  52.0 23.3 %collective-permute-start.8 = (bf16[192,1152]{1,0:T(8,128)(2,1)}, bf16[192,1152]{1,0:T(8,128)(2,1)S(1)}, u32[]{:S(2)}, u32[]{:S(2)}) collective-permute-start(bf16[192,1152]{1,0:T(8,128)(2,1)} %get-tuple-element.80), channel_id=1, source_target_pairs={{0,4},{2,6},{4,0},{6,2},{1,5},{3,7},{5,1},{7,3},{8,12},{10,14},{12... | collective-permute-start | bytes 1327112 | tf_op jit(solution)/shard_map/ppermute | solution.py:372
  53.8 21.5 %collective-permute-start.9 = (bf16[192,1152]{1,0:T(8,128)(2,1)}, bf16[192,1152]{1,0:T(8,128)(2,1)S(1)}, u32[]{:S(2)}, u32[]{:S(2)}) collective-permute-start(bf16[192,1152]{1,0:T(8,128)(2,1)} %get-tuple-element.80), channel_id=1, source_target_pairs={{0,6},{2,4},{4,2},{6,0},{1,7},{3,5},{5,3},{7,1},{8,14},{10,12},{12... | collective-permute-start | bytes 1327112 | tf_op jit(solution)/shard_map/ppermute | solution.py:372
  85.9 20.7 %collective-permute-start.11 = (bf16[1536,256]{1,0:T(8,128)(2,1)}, bf16[1536,256]{1,0:T(8,128)(2,1)S(1)}, u32[]{:S(2)}, u32[]{:S(2)}) collective-permute-start(bf16[1536,256]{1,0:T(8,128)(2,1)} %get-tuple-element.36.refs_1_.key_value), channel_id=1, source_target_pairs={{0,8},{8,0},{1,9},{9,1},{2,10},{10,2},{3,11},{11,3},{4,12},{12,4},... | collective-permute-start | bytes 2359304 | tf_op jit(solution)/shard_map/ppermute | solution.py:463
  88.2 42.1 %collective-permute-start.12 = (bf16[1536,256]{1,0:T(8,128)(2,1)}, bf16[1536,256]{1,0:T(8,128)(2,1)S(1)}, u32[]{:S(2)}, u32[]{:S(2)}) collective-permute-start(bf16[1536,256]{1,0:T(8,128)(2,1)} %get-tuple-element.38.refs_1_.key_value), channel_id=1, source_target_pairs={{0,8},{8,0},{1,9},{9,1},{2,10},{10,2},{3,11},{11,3},{4,12},{12,4},... | collective-permute-start | bytes 2359304 | tf_op jit(solution)/shard_map/ppermute | solution.py:463
  89.2 62.9 %collective-permute-start.13 = (bf16[1536,256]{1,0:T(8,128)(2,1)}, bf16[1536,256]{1,0:T(8,128)(2,1)S(1)}, u32[]{:S(2)}, u32[]{:S(2)}) collective-permute-start(bf16[1536,256]{1,0:T(8,128)(2,1)} %get-tuple-element.40.refs_1_.key_value), channel_id=1, source_target_pairs={{0,8},{8,0},{1,9},{9,1},{2,10},{10,2},{3,11},{11,3},{4,12},{12,4},... | collective-permute-start | bytes 2359304 | tf_op jit(solution)/shard_map/ppermute | solution.py:463
  168.3 10.5 %collective-permute-start.14 = (bf16[768,384]{1,0:T(8,128)(2,1)S(1)}, bf16[768,384]{1,0:T(8,128)(2,1)S(1)}, u32[]{:S(2)}, u32[]{:S(2)}) collective-permute-start(bf16[768,384]{1,0:T(8,128)(2,1)S(1)} %pad_maximum_fusion.6), channel_id=1, source_target_pairs={{0,1},{1,0},{2,3},{3,2},{4,5},{5,4},{6,7},{7,6},{8,9},{9,8},{10,11... | collective-permute-start | bytes 1769480 | tf_op jit(solution)/shard_map/ppermute | solution.py:399
  168.4 22.5 %collective-permute-start.16 = (bf16[768,768]{1,0:T(8,128)(2,1)}, bf16[768,768]{1,0:T(8,128)(2,1)}, u32[]{:S(2)}, u32[]{:S(2)}) collective-permute-start(bf16[768,768]{1,0:T(8,128)(2,1)} %bitcast.6), channel_id=1, source_target_pairs={{0,0},{1,16},{2,2},{3,18},{4,4},{5,20},{6,6},{7,22},{8,8},{9,24},{... | collective-permute-start | bytes 3538952 | tf_op jit(solution)/shard_map/ppermute | solution.py:428
  221.2 246.9 %reduce-scatter.8.cloned.1.call-start = ((), (), s32[]{:S(2)}) async-start(), calls=%async_computation.8 | async-start | bytes 1990656 | tf_op jit(solution)/shard_map/reduce_scatter | solution.py:542
  225.9 242.2 %reduce-scatter.6.cloned.1.call-start = ((), (), s32[]{:S(2)}) async-start(), calls=%async_computation.7 | async-start | bytes 3981312 | tf_op jit(solution)/shard_map/reduce_scatter | solution.py:542
  230.2 14.6 %collective-permute-start.17 = (bf16[768,384]{1,0:T(8,128)(2,1)}, bf16[768,384]{1,0:T(8,128)(2,1)}, u32[]{:S(2)}, u32[]{:S(2)}) collective-permute-start(bf16[768,384]{1,0:T(8,128)(2,1)} %get-tuple-element.87), channel_id=1, source_target_pairs={{0,1},{1,0},{2,3},{3,2},{4,5},{5,4},{6,7},{7,6},{8,9},{9,8},{10,11... | collective-permute-start | bytes 1769480 | tf_op jit(solution)/shard_map/ppermute | solution.py:399
  244.7 278.8 %all-reduce.3.cloned.1.call-start = ((), (), s32[]{:S(2)}) async-start(), calls=%async_computation.9 | async-start | bytes 1622016 | tf_op jit(solution)/shard_map/psum | solution.py:545
  278.5 65.3 %collective-permute-start.20 = (bf16[1536,256]{1,0:T(8,128)(2,1)}, bf16[1536,256]{1,0:T(8,128)(2,1)S(1)}, u32[]{:S(2)}, u32[]{:S(2)}) collective-permute-start(bf16[1536,256]{1,0:T(8,128)(2,1)} %get-tuple-element.59), channel_id=1, source_target_pairs={{0,8},{8,0},{1,9},{9,1},{2,10},{10,2},{3,11},{11,3},{4,12},{12,4},... | collective-permute-start | bytes 2359304 | tf_op jit(solution)/shard_map/ppermute | solution.py:507
  310.1 33.7 %collective-permute-start.19 = (bf16[1536,256]{1,0:T(8,128)(2,1)}, bf16[1536,256]{1,0:T(8,128)(2,1)S(1)}, u32[]{:S(2)}, u32[]{:S(2)}) collective-permute-start(bf16[1536,256]{1,0:T(8,128)(2,1)} %get-tuple-element.58), channel_id=1, source_target_pairs={{0,8},{8,0},{1,9},{9,1},{2,10},{10,2},{3,11},{11,3},{4,12},{12,4},... | collective-permute-start | bytes 2359304 | tf_op jit(solution)/shard_map/ppermute | solution.py:507
  328.1 20.2 %collective-permute-start.18 = (bf16[1536,256]{1,0:T(8,128)(2,1)}, bf16[1536,256]{1,0:T(8,128)(2,1)S(1)}, u32[]{:S(2)}, u32[]{:S(2)}) collective-permute-start(bf16[1536,256]{1,0:T(8,128)(2,1)} %get-tuple-element.57), channel_id=1, source_target_pairs={{0,8},{8,0},{1,9},{9,1},{2,10},{10,2},{3,11},{11,3},{4,12},{12,4},... | collective-permute-start | bytes 2359304 | tf_op jit(solution)/shard_map/ppermute | solution.py:507
  367.3 13.4 %collective-permute-start.23 = (bf16[192,1152]{1,0:T(8,128)(2,1)}, bf16[192,1152]{1,0:T(8,128)(2,1)}, u32[]{:S(2)}, u32[]{:S(2)}) collective-permute-start(bf16[192,1152]{1,0:T(8,128)(2,1)} %get-tuple-element.83), channel_id=1, source_target_pairs={{0,2},{2,0},{4,6},{6,4},{1,3},{3,1},{5,7},{7,5},{8,10},{10,8},{12,... | collective-permute-start | bytes 1327112 | tf_op jit(solution)/shard_map/ppermute | solution.py:387
  368.8 21.4 %collective-permute-start.24 = (bf16[192,1152]{1,0:T(8,128)(2,1)}, bf16[192,1152]{1,0:T(8,128)(2,1)}, u32[]{:S(2)}, u32[]{:S(2)}) collective-permute-start(bf16[192,1152]{1,0:T(8,128)(2,1)} %get-tuple-element.85), channel_id=1, source_target_pairs={{0,4},{2,6},{4,0},{6,2},{1,5},{3,7},{5,1},{7,3},{8,12},{10,14},{12... | collective-permute-start | bytes 1327112 | tf_op jit(solution)/shard_map/ppermute | solution.py:387
  369.7 20.5 %collective-permute-start.25 = (bf16[192,1152]{1,0:T(8,128)(2,1)}, bf16[192,1152]{1,0:T(8,128)(2,1)}, u32[]{:S(2)}, u32[]{:S(2)}) collective-permute-start(bf16[192,1152]{1,0:T(8,128)(2,1)} %get-tuple-element.84), channel_id=1, source_target_pairs={{0,6},{2,4},{4,2},{6,0},{1,7},{3,5},{5,3},{7,1},{8,14},{10,12},{12... | collective-permute-start | bytes 1327112 | tf_op jit(solution)/shard_map/ppermute | solution.py:387
  391.8 7.1 %collective-permute-start.26 = (bf16[48,1152]{1,0:T(8,128)(2,1)S(1)}, bf16[48,1152]{1,0:T(8,128)(2,1)S(1)}, u32[]{:S(2)}, u32[]{:S(2)}) collective-permute-start(bf16[48,1152]{1,0:T(8,128)(2,1)S(1)} %get-tuple-element.92), channel_id=1, source_target_pairs={{0,8},{8,0},{16,24},{24,16},{1,9},{9,1},{17,25},{25,17},{2,10},{10... | collective-permute-start | bytes 331784 | tf_op jit(solution)/shard_map/ppermute | solution.py:387
  393.2 9.3 %collective-permute-start.27 = (bf16[48,1152]{1,0:T(8,128)(2,1)S(1)}, bf16[48,1152]{1,0:T(8,128)(2,1)S(1)}, u32[]{:S(2)}, u32[]{:S(2)}) collective-permute-start(bf16[48,1152]{1,0:T(8,128)(2,1)S(1)} %get-tuple-element.94), channel_id=1, source_target_pairs={{0,16},{8,24},{16,0},{24,8},{1,17},{9,25},{17,1},{25,9},{2,18},{10... | collective-permute-start | bytes 331784 | tf_op jit(solution)/shard_map/ppermute | solution.py:387
  393.2 9.3 %collective-permute-start.28 = (bf16[48,1152]{1,0:T(8,128)(2,1)S(1)}, bf16[48,1152]{1,0:T(8,128)(2,1)S(1)}, u32[]{:S(2)}, u32[]{:S(2)}) collective-permute-start(bf16[48,1152]{1,0:T(8,128)(2,1)S(1)} %get-tuple-element.93), channel_id=1, source_target_pairs={{0,24},{8,16},{16,8},{24,0},{1,25},{9,17},{17,9},{25,1},{2,26},{10... | collective-permute-start | bytes 331784 | tf_op jit(solution)/shard_map/ppermute | solution.py:387
  396.4 59.5 %collective-permute-start.21 = (bf16[768,768]{1,0:T(8,128)(2,1)S(1)}, bf16[768,768]{1,0:T(8,128)(2,1)S(1)}, u32[]{:S(2)}, u32[]{:S(2)}) collective-permute-start(bf16[768,768]{1,0:T(8,128)(2,1)S(1)} %slice.85), channel_id=1, source_target_pairs={{0,1},{1,0},{2,3},{3,2},{4,5},{5,4},{6,7},{7,6},{8,9},{9,8},{10,11... | collective-permute-start | bytes 3538952 | tf_op jit(solution)/shard_map/ppermute | solution.py:399
  402.6 53.3 %copy-start.16 = (f32[768]{0:T(1024)S(1)}, f32[768]{0:T(1024)}, u32[]{:S(2)}) copy-start(f32[768]{0:T(1024)} %get-tuple-element.68) | copy-start | bytes 9220
  402.6 19.1 %collective-permute-start.29 = (f32[48,1152]{1,0:T(8,128)S(1)}, f32[48,1152]{1,0:T(8,128)S(1)}, u32[]{:S(2)}, u32[]{:S(2)}) collective-permute-start(f32[48,1152]{1,0:T(8,128)S(1)} %get-tuple-element.74), channel_id=1, source_target_pairs={{0,8},{8,0},{16,24},{24,16},{1,9},{9,1},{17,25},{25,17},{2,10},{10... | collective-permute-start | bytes 663560 | tf_op jit(solution)/shard_map/ppermute | solution.py:372
  409.0 68.7 %collective-permute-start.15 = (bf16[768,768]{1,0:T(8,128)(2,1)}, bf16[768,768]{1,0:T(8,128)(2,1)}, u32[]{:S(2)}, u32[]{:S(2)}) collective-permute-start(bf16[768,768]{1,0:T(8,128)(2,1)} %add_convert_fusion.2), channel_id=1, source_target_pairs={{0,0},{1,16},{2,2},{3,18},{4,4},{5,20},{6,6},{7,22},{8,8},{9,24},{... | collective-permute-start | bytes 3538952 | tf_op jit(solution)/shard_map/ppermute | solution.py:555
  419.4 36.4 %collective-permute-start.30 = (f32[48,1152]{1,0:T(8,128)S(1)}, f32[48,1152]{1,0:T(8,128)S(1)}, u32[]{:S(2)}, u32[]{:S(2)}) collective-permute-start(f32[48,1152]{1,0:T(8,128)S(1)} %get-tuple-element.74), channel_id=1, source_target_pairs={{0,16},{8,24},{16,0},{24,8},{1,17},{9,25},{17,1},{25,9},{2,18},{10... | collective-permute-start | bytes 663560 | tf_op jit(solution)/shard_map/ppermute | solution.py:372
  419.4 36.4 %collective-permute-start.31 = (f32[48,1152]{1,0:T(8,128)S(1)}, f32[48,1152]{1,0:T(8,128)S(1)}, u32[]{:S(2)}, u32[]{:S(2)}) collective-permute-start(f32[48,1152]{1,0:T(8,128)S(1)} %get-tuple-element.74), channel_id=1, source_target_pairs={{0,24},{8,16},{16,8},{24,0},{1,25},{9,17},{17,9},{25,1},{2,26},{10... | collective-permute-start | bytes 663560 | tf_op jit(solution)/shard_map/ppermute | solution.py:372
  458.6 5.3 collective-permute-start.33
  462.0 49.9 %collective-permute-start.22 = (bf16[768,768]{1,0:T(8,128)(2,1)}, bf16[768,768]{1,0:T(8,128)(2,1)S(1)}, u32[]{:S(2)}, u32[]{:S(2)}) collective-permute-start(bf16[768,768]{1,0:T(8,128)(2,1)} %add_convert_fusion.1), channel_id=1, source_target_pairs={{0,0},{1,16},{2,2},{3,18},{4,4},{5,20},{6,6},{7,22},{8,8},{9,24},{... | collective-permute-start | bytes 3538952 | tf_op jit(solution)/shard_map/ppermute | solution.py:556
  464.6 4.8 collective-permute-start.34
  466.1 5.8 %collective-permute-start.35 = (f32[2,768]{1,0:T(2,128)S(1)}, f32[2,768]{1,0:T(2,128)S(1)}, u32[]{:S(2)}, u32[]{:S(2)}) collective-permute-start(f32[2,768]{1,0:T(2,128)S(1)} %fusion.27), channel_id=1, source_target_pairs={{0,4},{2,6},{4,0},{6,2},{1,5},{3,7},{5,1},{7,3},{8,12},{10,14},{12... | collective-permute-start | bytes 18440 | tf_op jit(solution)/shard_map/ppermute | solution.py:395
  467.3 4.7 collective-permute-start.36
  469.4 39.2 %collective-permute-start.32 = (f32[96,1152]{1,0:T(8,128)S(1)}, f32[96,1152]{1,0:T(8,128)S(1)}, u32[]{:S(2)}, u32[]{:S(2)}) collective-permute-start(f32[96,1152]{1,0:T(8,128)S(1)} %get-tuple-element.89), channel_id=1, source_target_pairs={{0,1},{1,0},{2,3},{3,2},{4,5},{5,4},{6,7},{7,6},{8,9},{9,8},{10,11... | collective-permute-start | bytes 1327112 | tf_op jit(solution)/shard_map/ppermute | solution.py:399
  472.0 6.3 %collective-permute-start.37 = (f32[2,768]{1,0:T(2,128)S(1)}, f32[2,768]{1,0:T(2,128)S(1)}, u32[]{:S(2)}, u32[]{:S(2)}) collective-permute-start(f32[2,768]{1,0:T(2,128)S(1)} %add_add_fusion.3), channel_id=1, source_target_pairs={{0,8},{8,0},{16,24},{24,16},{1,9},{9,1},{17,25},{25,17},{2,10},{10... | collective-permute-start | bytes 18440 | tf_op jit(solution)/shard_map/ppermute | solution.py:395
  474.8 33.2 %collective-permute-start.38 = (f32[2,768]{1,0:T(2,128)S(1)}, f32[2,768]{1,0:T(2,128)S(1)}, u32[]{:S(2)}, u32[]{:S(2)}) collective-permute-start(f32[2,768]{1,0:T(2,128)S(1)} %add_add_fusion.3), channel_id=1, source_target_pairs={{0,16},{8,24},{16,0},{24,8},{1,17},{9,25},{17,1},{25,9},{2,18},{10... | collective-permute-start | bytes 18440 | tf_op jit(solution)/shard_map/ppermute | solution.py:395
  477.8 30.2 %collective-permute-start.39 = (f32[2,768]{1,0:T(2,128)S(1)}, f32[2,768]{1,0:T(2,128)S(1)}, u32[]{:S(2)}, u32[]{:S(2)}) collective-permute-start(f32[2,768]{1,0:T(2,128)S(1)} %add_add_fusion.3), channel_id=1, source_target_pairs={{0,24},{8,16},{16,8},{24,0},{1,25},{9,17},{17,9},{25,1},{2,26},{10... | collective-permute-start | bytes 18440 | tf_op jit(solution)/shard_map/ppermute | solution.py:395
  (32 other events, 292.1 us)
Sparse Core Ops, SparseCore 0:
  9.9 28.3 all-gather.3
  40.2 47.4 all-gather.5
  89.5 26.5 all-gather.7
  221.3 46.5 reduce-scatter.3
  271.5 39.3 reduce-scatter.7
  314.7 48.0 reduce-scatter.5
  468.3 55.2 all-reduce.2
